TPU v7x, 32 devices: a whole 2x2x4 slice. The times are simulated.
32 devices in a mesh: dp: 8 (over z, y), tm: 4 (over x, core).
Axes of the slice: x: 2, y: 2, z: 4, core: 2. Of those that a mesh axis runs over, the one named last changes fastest.
Arguments:
- frames: bfloat16 [8, 3072, 1536], P('dp', 'tm')
- w_qkv: bfloat16 [1536, 2304], P('dp'), may hold values from -0.15625 to 0.15625
- utt_start: int32 [8, 3], P('dp'), may hold values from 0 to 2943, as said below
- stretch_utt: int32 [8, 12], P('dp'), may hold values from 0 to 2, as said below
- left_stretches: int32 [8, 12], P('dp'), may hold values from 0 to 2, as said below
Outputs:
- context: bfloat16 [8, 3072, 768], P('dp', 'tm')
Inputs may be any that keep to these rules, and one draw needn't show every extreme that they name: `stretch_utt`: in each pack nondecreasing along blocks; utterance u covers one or more whole consecutive blocks; every utterance of 0 to 2 occurs, block 0 in utterance 0. `utt_start`: for utterance u with first block b, at least 256 * b and less than 256 * b + 128. `left_stretches`: at most the number of earlier blocks of the same utterance.
All inputs are finite; a program needn't handle non-finite values.
Results may differ from a plain program's by a relative error of at most 0.0045.
The roundings to bfloat16 on the way count: a program that leaves them out, or rounds other values in their place, can miss the bound.
Values may be sent and summed in bfloat16 or wider, within the bound.
No kernel may reach another device: no remote copies, remote signals or barrier semaphores. Data moves between devices by JAX's collectives and lax.ppermute only.
A program may use at most 64 MiB of HBM per device.

v0:
```python
import functools
import math

import jax
import jax.numpy as jnp
from jax import lax
from jax.experimental import pallas as pl
from jax.experimental.pallas import tpu as pltpu
from jax.sharding import PartitionSpec as P

HEAD_DIM = 96
STRETCH = 256
LEFT = 2
LANES = 128
GROUPS = 4
EXP_SCALE = HEAD_DIM**-0.5 * math.log2(math.e)
REACH = LEFT * STRETCH
MIB = 1024 * 1024


def dot(a, b, dims=((1,), (0,))):
    return lax.dot_general(a, b, (dims, ((), ())), preferred_element_type=jnp.float32)


def head_window(head):
    first = head * HEAD_DIM // LANES * LANES
    last = -(-(head + 1) * HEAD_DIM // LANES) * LANES
    return first, last


def start_all(sems, pairs):
    copies = []
    for i, (*source, target) in enumerate(pairs):
        if len(source) == 1:
            copy = pltpu.make_async_copy(source[0], target, sems.at[i])
            copy.start()
        else:
            for n, choice in enumerate(source[0]):
                copy = pltpu.make_async_copy(choice, target, sems.at[i])
                pl.when(source[1] == n)(copy.start)
        copies.append(copy)
    return copies


class Blocks:
    def __init__(self, blocks, n_late, find):
        self.operands = [operand for block in blocks for operand in block]
        self.counts = [len(block) for block in blocks]
        self.rows = [block[0].shape[0] for block in blocks]
        self.n_late = n_late
        self.early_operands = self.operands[: sum(self.counts[:-n_late])]
        self.find = find

    def copies(self, refs, found, members, target, first=0, columns=slice(None)):
        pairs = []
        for i in members:
            at = sum(self.counts[:i])
            choices = [ref.at[:, columns] for ref in refs[at : at + self.counts[i]]]
            row, which = found[i]
            goal = target.at[pl.ds(pl.multiple_of(row - first, self.rows[i]), self.rows[i])]
            pairs.append((choices[0], goal) if len(choices) == 1 else (choices, which, goal))
        return pairs


def early_kernel(blocks, *refs):
    n = len(blocks.early_operands)
    own_ref, partner_ref, own_sum, partner_sum, w_s, own_s, partner_s, sems = refs[n:]
    found, late_first = blocks.find()
    depth = w_s.shape[0]
    first = jnp.where(late_first == 0, own_ref.shape[1] - depth, 0)
    members = range(len(found) - blocks.n_late)
    pairs = blocks.copies(refs, found, members, w_s, first)
    columns = pl.ds(pl.multiple_of(first, LANES), depth)
    pairs.append((own_ref.at[:, columns], own_s))
    pairs.append((partner_ref.at[:, columns], partner_s))
    for copy in start_all(sems, pairs):
        copy.wait()
    width = w_s.shape[1] // 3
    for x_s, out in ((own_s, own_sum), (partner_s, partner_sum)):
        for third in range(3):
            cols = slice(third * width, (third + 1) * width)
            out[:, cols] = dot(x_s[...], w_s[:, cols])


def late_kernel(blocks, start_ref, owner_ref, left_ref, *refs):
    n = len(blocks.operands)
    own_ref, partner_ref, halo_ref, own_sum, partner_sum = refs[n : n + 5]
    out_ref, q_own, k_out, v_out, kv_out, q_partner, w_s, own_s, partner_s, sems = refs[n + 5 :]
    depth = w_s.shape[0]
    width = w_s.shape[1] // 3
    rows = own_s.shape[0]
    core = lax.axis_index("tm") % 2
    found, late_first = blocks.find()
    everything = range(len(found))
    pairs = blocks.copies(refs, found, everything[-blocks.n_late :], w_s, late_first)
    columns = pl.ds(pl.multiple_of(late_first, LANES), depth)
    pairs.append((partner_ref.at[:, columns], partner_s))
    pairs.append((own_ref.at[:, columns], own_s))
    n_first = len(pairs)
    pairs += blocks.copies(refs, found, everything, kv_out, 0, slice(width, 3 * width))
    copies = start_all(sems, pairs)
    for copy in copies[:n_first]:
        copy.wait()
    for x_s, acc, query, place in (
        (partner_s, partner_sum, q_partner, 1 - core),
        (own_s, own_sum, q_own, core),
    ):
        row = pl.multiple_of(place * rows + REACH, STRETCH)
        for third, dst in enumerate((query, k_out, v_out)):
            cols = slice(third * width, (third + 1) * width)
            value = (acc[:, cols] + dot(x_s[...], w_s[:, cols])).astype(jnp.bfloat16)
            if third == 0:
                dst[...] = value
            else:
                dst[pl.ds(row, rows), :] = value
    for copy in copies[n_first:]:
        copy.wait()

    @pl.when(core == 1)
    def _():
        k_out[:REACH, :] = dot(halo_ref[...], kv_out[:, :width]).astype(jnp.bfloat16)
        v_out[:REACH, :] = dot(halo_ref[...], kv_out[:, width:]).astype(jnp.bfloat16)

    first = pl.multiple_of((1 - core) * rows, STRETCH)
    attend(start_ref, owner_ref, left_ref, 1 - core, q_partner, 0, k_out, v_out, first, out_ref)


def own_kernel(
    start_ref, owner_ref, left_ref, q_ref, k_ref, v_ref, kv_ref, halo_ref, out_ref, k_s, v_s
):
    rows, width = out_ref.shape
    core = lax.axis_index("tm") % 2
    own = pl.multiple_of(core * rows + REACH, STRETCH)
    k_s[REACH:, :] = k_ref[pl.ds(own, rows), :]
    v_s[REACH:, :] = v_ref[pl.ds(own, rows), :]

    @pl.when(core == 0)
    def _():
        k_s[:REACH, :] = dot(halo_ref[...], kv_ref[:, :width]).astype(jnp.bfloat16)
        v_s[:REACH, :] = dot(halo_ref[...], kv_ref[:, width:]).astype(jnp.bfloat16)

    @pl.when(core == 1)
    def _():
        k_s[:REACH, :] = k_ref[rows : rows + REACH, :]
        v_s[:REACH, :] = v_ref[rows : rows + REACH, :]

    attend(start_ref, owner_ref, left_ref, core, q_ref, 0, k_s, v_s, 0, out_ref)


def attend(start_ref, owner_ref, left_ref, place, q_s, q_first, k_s, v_s, k_first, out_ref):
    rows, width = out_ref.shape
    chunks = rows // STRETCH
    pair = lax.axis_index("tm") // 2
    lane = lax.broadcasted_iota(jnp.int32, (1, width), 1)
    heads = width // HEAD_DIM

    def attend_block(chunk, start, lowest, q_row, k_row, span, out_ref, out_row):
        first_key = (chunk + 1) * STRETCH - span
        key_frame = first_key + lax.broadcasted_iota(jnp.int32, (1, STRETCH), 1)
        bias = jnp.where(key_frame >= lowest, 0.0, -jnp.inf).astype(jnp.float32)
        frame = chunk * STRETCH + lax.broadcasted_iota(jnp.int32, (STRETCH, 1), 0)
        live = frame >= start
        windows = [head_window(head) for head in range(heads)]
        insides = [
            ((lane >= head * HEAD_DIM) & (lane < (head + 1) * HEAD_DIM))[:, first:last]
            for head, (first, last) in enumerate(windows)
        ]
        tiles = [jnp.zeros((STRETCH, LANES), jnp.float32) for _ in range(width // LANES)]

        def score(head):
            first, last = windows[head]
            q = q_s[pl.ds(q_row, STRETCH), first:last]
            q = jnp.where(insides[head], q, jnp.zeros_like(q))
            return dot(q, k_s[pl.ds(k_row, span), first:last], ((1,), (1,)))

        def weigh(scores):
            scores = [scores[:, at : at + STRETCH] for at in range(0, span, STRETCH)]
            scores[0] = scores[0] + bias
            top = functools.reduce(jnp.maximum, scores)
            top = jnp.max(top, axis=-1, keepdims=True)
            expo = [jnp.exp2((part - top) * EXP_SCALE) for part in scores]
            total = jnp.sum(functools.reduce(jnp.add, expo), axis=-1, keepdims=True)
            share = 1.0 / total
            return jnp.concatenate([(part * share).astype(jnp.bfloat16) for part in expo], axis=1)

        def mix(head, probs):
            first, last = windows[head]
            mixed = dot(probs, v_s[pl.ds(k_row, span), first:last])
            for tile in range(first // LANES, last // LANES):
                at = tile * LANES - first
                tiles[tile] = jnp.where(
                    insides[head][:, at : at + LANES], mixed[:, at : at + LANES], tiles[tile]
                )

        scores = score(0)
        probs = None
        for head in range(heads):
            following = score(head + 1) if head + 1 < heads else None
            weighed = weigh(scores)
            if probs is not None:
                mix(head - 1, probs)
            scores, probs = following, weighed
        mix(heads - 1, probs)
        for tile, value in enumerate(tiles):
            value = jnp.where(live, value, 0.0).astype(jnp.bfloat16)
            out_ref[pl.ds(out_row, STRETCH), tile * LANES : (tile + 1) * LANES] = value

    @pl.loop(0, chunks)
    def _(i):
        row = pl.multiple_of(i * STRETCH, STRETCH)
        chunk = (pair * 2 + place) * chunks + i
        left = left_ref[0, chunk]
        start = start_ref[0, owner_ref[0, chunk]]
        lowest = jnp.maximum((chunk - left) * STRETCH, start)
        for back in range(LEFT + 1):

            @pl.when(left == back)
            def _():
                q_row = pl.multiple_of(q_first + row, STRETCH)
                k_row = pl.multiple_of(k_first + row + (LEFT - back) * STRETCH, STRETCH)
                attend_block(chunk, start, lowest, q_row, k_row, (back + 1) * STRETCH, out_ref, row)


def after(value, *others):
    return lax.optimization_barrier((value, *others))[0]


SMEM_SPEC = pl.BlockSpec(memory_space=pltpu.SMEM)
VMEM_SPEC = pl.BlockSpec(memory_space=pltpu.VMEM)
ANY_SPEC = pl.BlockSpec(memory_space=pl.ANY)


def project_early(blocks, inputs, partner):
    rows, depth = inputs.shape
    depth -= depth // GROUPS
    cols = blocks.operands[0].shape[1]
    n_copies = len(blocks.counts) - blocks.n_late + 2
    return pl.pallas_call(
        functools.partial(early_kernel, blocks),
        out_shape=[jax.ShapeDtypeStruct((rows, cols), jnp.float32)] * 2,
        in_specs=[ANY_SPEC] * (len(blocks.early_operands) + 2),
        out_specs=[VMEM_SPEC] * 2,
        scratch_shapes=[
            pltpu.VMEM((depth, cols), jnp.bfloat16),
            pltpu.VMEM((rows, depth), jnp.bfloat16),
            pltpu.VMEM((rows, depth), jnp.bfloat16),
            pltpu.SemaphoreType.DMA((n_copies,)),
        ],
        compiler_params=pltpu.CompilerParams(vmem_limit_bytes=24 * MIB),
        cost_estimate=pl.CostEstimate(flops=0, bytes_accessed=0, transcendentals=0),
        name="project_early",
    )(*blocks.early_operands, inputs, partner)


def tail_kernel(x_ref, out_ref, sems):
    rows = out_ref.shape[0]
    for copy in start_all(sems, [(x_ref.at[x_ref.shape[0] - rows :, :], out_ref)]):
        copy.wait()


def take_tail(x):
    return pl.pallas_call(
        tail_kernel,
        out_shape=jax.ShapeDtypeStruct((REACH, x.shape[1]), x.dtype),
        in_specs=[ANY_SPEC],
        out_specs=VMEM_SPEC,
        scratch_shapes=[pltpu.SemaphoreType.DMA((1,))],
        compiler_params=pltpu.CompilerParams(vmem_limit_bytes=4 * MIB),
        name="take_tail",
    )(x)


def project_late_attend(tables, blocks, inputs, partner, halo, sums):
    rows, depth = inputs.shape
    late_depth = depth // GROUPS
    cols = blocks.operands[0].shape[1]
    width = cols // 3
    keys = jax.ShapeDtypeStruct((2 * rows + REACH, width), jnp.bfloat16)
    queries = jax.ShapeDtypeStruct((rows, width), jnp.bfloat16)
    return pl.pallas_call(
        functools.partial(late_kernel, blocks),
        out_shape=[
            queries,
            queries,
            keys,
            keys,
            jax.ShapeDtypeStruct((depth, 2 * width), jnp.bfloat16),
        ],
        in_specs=[SMEM_SPEC] * 3 + [ANY_SPEC] * (len(blocks.operands) + 2) + [VMEM_SPEC] * 3,
        out_specs=[VMEM_SPEC] * 5,
        scratch_shapes=[
            pltpu.VMEM((rows, width), jnp.bfloat16),
            pltpu.VMEM((late_depth, cols), jnp.bfloat16),
            pltpu.VMEM((rows, late_depth), jnp.bfloat16),
            pltpu.VMEM((rows, late_depth), jnp.bfloat16),
            pltpu.SemaphoreType.DMA((len(blocks.counts) + blocks.n_late + 2,)),
        ],
        compiler_params=pltpu.CompilerParams(vmem_limit_bytes=24 * MIB),
        name="project_late_attend",
    )(*tables, *blocks.operands, inputs, partner, halo, *sums)


def attend_own(tables, query, keys, values, weights, halo):
    rows, width = query.shape
    return pl.pallas_call(
        own_kernel,
        out_shape=jax.ShapeDtypeStruct((rows, width), jnp.bfloat16),
        in_specs=[SMEM_SPEC] * 3 + [VMEM_SPEC] * 5,
        out_specs=VMEM_SPEC,
        scratch_shapes=[pltpu.VMEM((rows + REACH, width), jnp.bfloat16)] * 2,
        compiler_params=pltpu.CompilerParams(vmem_limit_bytes=20 * MIB),
        name="attend_own",
    )(*tables, query, keys, values, weights, halo)


def gather_neighbours(half):
    size = half.shape[0]

    def along(name, block, hops):
        with jax.named_scope(name):
            return lax.ppermute(
                block, "dp", [(2 * a + s, 2 * b + s) for a, b in hops for s in range(2)]
            )

    def across(name, block, places):
        with jax.named_scope(name):
            return lax.ppermute(
                block, "dp", [(2 * a + s, 2 * a + 1 - s) for a in places for s in range(2)]
            )

    line, ends, middles = range(4), (0, 3), (1, 2)
    outward = [(1, 0), (2, 3)]
    between = [(1, 2), (2, 1)]
    near = along("near", half, outward + [(0, 1), (3, 2)])
    mid = along("mid", half, between)
    half_across = across("half_across", half, line)
    mid_far = along("mid_far", near, between)
    near_across = across("near_across", after(near, half_across, mid), line)
    end_mid = along("end_mid", mid, outward)
    mid_across = across("mid_across", after(mid, near_across, mid_far), middles)
    end_mid_across = across("end_mid_across", after(end_mid, near_across), ends)
    end_far = along("end_far", after(mid_far, end_mid), outward)
    mid_far_across = across("mid_far_across", after(mid_far, mid_across, end_far), middles)
    end_far_across = across("end_far_across", after(end_far, end_mid_across), ends)

    def find():
        index = lax.axis_index("dp")
        place, side = index // 2, index % 2
        is_end = jnp.where((place == 0) | (place == 3), 1, 0)
        second = jnp.where(is_end == 1, place ^ 2, 3 - place)
        third = jnp.where(is_end == 1, 3 - place, place ^ 2)
        spots = (place, place ^ 1, second, third)
        found = [((2 * spot + (side ^ n)) * size, is_end) for spot in spots for n in range(2)]
        return found, third * 2 * size

    blocks = [
        (half,),
        (half_across,),
        (near,),
        (near_across,),
        (mid, end_mid),
        (mid_across, end_mid_across),
        (mid_far, end_far),
        (mid_far_across, end_far_across),
    ]
    marks = (
        (near_across, mid_far, end_mid),
        (mid_across, end_mid_across, end_far),
        (mid_far_across, end_far_across),
    )
    return Blocks(blocks, 2, find), marks


def local(frames, w_qkv, utt_start, stretch_utt, left_stretches):
    inputs = frames[0]
    depth = inputs.shape[1]
    members = lax.axis_size("tm")
    core = lax.axis_index("tm") % 2

    inner = w_qkv.shape[1] // 3
    width = inner // 2
    thirds = [w_qkv[:, i * inner : (i + 1) * inner] for i in range(3)]
    half = jnp.concatenate(
        [jnp.where(core == 0, third[:, :width], third[:, width:]) for third in thirds], axis=1
    )

    tail = take_tail(after(inputs, half))
    with jax.named_scope("partner"):
        partner = lax.ppermute(inputs, "tm", [(i, i ^ 1) for i in range(members)])
    if lax.axis_size("dp") == 8:
        blocks, marks = gather_neighbours(half)
    else:
        weights = lax.all_gather(half, "dp", axis=0, tiled=True)
        late_first = depth - depth // GROUPS
        found = [(0, 0), (late_first, 0)], late_first
        parts = [(weights[:late_first],), (weights[late_first:],)]
        blocks, marks = Blocks(parts, 1, lambda: found), ((half,),) * 3

    with jax.named_scope("halo"):
        halo = lax.ppermute(
            after(tail, *marks[0]), "tm", [(i, i + 2) for i in range(1, members - 2, 2)]
        )

    tables = (utt_start, stretch_utt, left_stretches)
    sums = project_early(blocks, inputs, partner)
    with jax.named_scope("halo_first"):
        halo_first = lax.ppermute(
            after(halo, *marks[2], *sums), "tm", [(i + 1, i) for i in range(0, members, 2)]
        )
    partner_out, query, keys, values, weights = project_late_attend(
        tables, blocks, inputs, partner, halo, sums
    )
    with jax.named_scope("swap"):
        other = lax.ppermute(partner_out, "tm", [(i, i ^ 1) for i in range(members)])
    own_out = attend_own(tables, query, keys, values, weights, halo_first)
    left = jnp.where(core == 0, own_out, other)
    right = jnp.where(core == 0, other, own_out)
    return jnp.concatenate([left, right], axis=1)[None]


def solution(mesh):
    return jax.shard_map(
        local,
        mesh=mesh,
        in_specs=(P("dp", "tm", None), P("dp", None), P("dp", None), P("dp", None), P("dp", None)),
        out_specs=P("dp", "tm", None),
        check_vma=False,
    )
```

profile of v0, /device:TPU:0, one launch (start us, length us, event | category | flops | bytes accessed | tf_op | source)
XLA Modules:
  0.0 79.0 jit_solution(13003065887821194197)
XLA Ops:
  0.0 1.3 %slice_select_fusion.2 = (bf16[192,384]{1,0:T(8,128)(2,1)S(1)}, bf16[192,384]{1,0:T(8,128)(2,1)S(1)}, bf16[192,384]{1,0:T(8,128)(2,1)S(1)}) fusion(bf16[192,2304]{1,0:T(8,128)(2,1)} %param.6, pred[]{:T(512)S(6)} %eq.4), kind=kLoop, calls=%fused_computation.6 | loop fusion | flops 221184 | bytes 1327105 | tf_op jit(solution)/shard_map/jit(_where)/select_n | solution.py:384
  1.4 0.7 collective-permute-start.2
  2.1 5.9 %collective-permute-start.1 = (bf16[192,1152]{1,0:T(8,128)(2,1)S(1)}, bf16[192,1152]{1,0:T(8,128)(2,1)S(1)}, u32[]{:S(2)}, u32[]{:S(2)}) collective-permute-start(bf16[192,1152]{1,0:T(8,128)(2,1)S(1)} %pad_maximum_fusion.refs_0_), channel_id=1, source_target_pairs={{8,0},{12,4},{16,24},{20,28},{0,8},{4,12},{24,16},{28,20},{9,1},{1... | collective-permute-start | bytes 1327112 | tf_op jit(solution)/shard_map/near/ppermute | solution.py:321
  7.9 1.5 %collective-permute-start = (bf16[192,1152]{1,0:T(8,128)(2,1)S(1)}, bf16[192,1152]{1,0:T(8,128)(2,1)S(1)}, u32[]{:S(2)}, u32[]{:S(2)}) collective-permute-start(bf16[192,1152]{1,0:T(8,128)(2,1)S(1)} %pad_maximum_fusion.refs_0_), channel_id=1, source_target_pairs={{0,4},{4,0},{8,12},{12,8},{16,20},{20,16},{24,28},{28,24},{1,5},{5... | collective-permute-start | bytes 1327112 | tf_op jit(solution)/shard_map/half_across/ppermute | solution.py:327
  9.5 0.0 collective-permute-start.11
  9.5 0.0 collective-permute-done.2.refs_4_
  9.5 8.4 %collective-permute-done.1.refs_2_ = bf16[192,1152]{1,0:T(8,128)(2,1)S(1)} collective-permute-done((bf16[192,1152]{1,0:T(8,128)(2,1)S(1)}, bf16[192,1152]{1,0:T(8,128)(2,1)S(1)}, u32[]{:S(2)}, u32[]{:S(2)}) %collective-permute-start.1) | collective-permute-done | bytes 442400 | tf_op jit(solution)/shard_map/near/ppermute | solution.py:321
  17.8 1.5 %collective-permute-done.refs_1_ = bf16[192,1152]{1,0:T(8,128)(2,1)S(1)} collective-permute-done((bf16[192,1152]{1,0:T(8,128)(2,1)S(1)}, bf16[192,1152]{1,0:T(8,128)(2,1)S(1)}, u32[]{:S(2)}, u32[]{:S(2)}) %collective-permute-start) | collective-permute-done | bytes 442400 | tf_op jit(solution)/shard_map/half_across/ppermute | solution.py:327
  19.3 1.3 %collective-permute-start.4 = (bf16[192,1152]{1,0:T(8,128)(2,1)S(1)}, bf16[192,1152]{1,0:T(8,128)(2,1)S(1)}, u32[]{:S(2)}, u32[]{:S(2)}) collective-permute-start(bf16[192,1152]{1,0:T(8,128)(2,1)S(1)} %collective-permute-done.2.refs_4_), channel_id=1, source_target_pairs={{8,0},{12,4},{16,24},{20,28},{9,1},{13,5},{17,25},{21,29},{10,2},{... | collective-permute-start | bytes 1327112 | tf_op jit(solution)/shard_map/end_mid/ppermute | solution.py:321
  20.6 0.7 collective-permute-start.5
  21.3 1.6 %collective-permute-start.3 = (bf16[192,1152]{1,0:T(8,128)(2,1)S(1)}, bf16[192,1152]{1,0:T(8,128)(2,1)S(1)}, u32[]{:S(2)}, u32[]{:S(2)}) collective-permute-start(bf16[192,1152]{1,0:T(8,128)(2,1)S(1)} %collective-permute-done.1.refs_2_), channel_id=1, source_target_pairs={{0,4},{4,0},{8,12},{12,8},{16,20},{20,16},{24,28},{28,24},{1,5},{5... | collective-permute-start | bytes 1327112 | tf_op jit(solution)/shard_map/near_across/ppermute | solution.py:327
  22.9 0.0 copy-start
  22.9 1.7 %copy-done = bf16[1,768,1536]{2,1,0:T(8,128)(2,1)S(1)} copy-done((bf16[1,768,1536]{2,1,0:T(8,128)(2,1)S(1)}, bf16[1,768,1536]{2,1,0:T(8,128)(2,1)}, u32[]{:S(2)}) %copy-start) | copy-done | bytes 2359320
  24.5 0.0 copy-start.1
  24.5 0.1 take_tail.1
  24.7 0.0 copy-start.2
  24.7 0.0 copy-start.3
  24.7 0.0 copy-start.4
  24.7 6.9 %collective-permute-done.4.refs_5_ = bf16[192,1152]{1,0:T(8,128)(2,1)S(1)} collective-permute-done((bf16[192,1152]{1,0:T(8,128)(2,1)S(1)}, bf16[192,1152]{1,0:T(8,128)(2,1)S(1)}, u32[]{:S(2)}, u32[]{:S(2)}) %collective-permute-start.4) | collective-permute-done | bytes 442400 | tf_op jit(solution)/shard_map/end_mid/ppermute | solution.py:321
  31.6 0.0 collective-permute-done.5.refs_8_
  31.6 0.2 collective-permute-done.3.refs_3_
  31.8 0.8 collective-permute-start.12
  32.5 1.3 %collective-permute-start.8 = (bf16[192,1152]{1,0:T(8,128)(2,1)S(1)}, bf16[192,1152]{1,0:T(8,128)(2,1)S(1)}, u32[]{:S(2)}, u32[]{:S(2)}) collective-permute-start(bf16[192,1152]{1,0:T(8,128)(2,1)S(1)} %collective-permute-done.5.refs_8_), channel_id=1, source_target_pairs={{8,0},{12,4},{16,24},{20,28},{9,1},{13,5},{17,25},{21,29},{10,2},{... | collective-permute-start | bytes 1327112 | tf_op jit(solution)/shard_map/end_far/ppermute | solution.py:321
  33.8 0.7 collective-permute-start.6
  34.5 3.4 %collective-permute-start.7 = (bf16[192,1152]{1,0:T(8,128)(2,1)S(1)}, bf16[192,1152]{1,0:T(8,128)(2,1)S(1)}, u32[]{:S(2)}, u32[]{:S(2)}) collective-permute-start(bf16[192,1152]{1,0:T(8,128)(2,1)S(1)} %collective-permute-done.4.refs_5_), channel_id=1, source_target_pairs={{0,4},{4,0},{24,28},{28,24},{1,5},{5,1},{25,29},{29,25},{2,6},{6,2... | collective-permute-start | bytes 1327112 | tf_op jit(solution)/shard_map/end_mid_across/ppermute | solution.py:327
  38.0 9.3 %collective-permute-done.8.refs_9_ = bf16[192,1152]{1,0:T(8,128)(2,1)S(1)} collective-permute-done((bf16[192,1152]{1,0:T(8,128)(2,1)S(1)}, bf16[192,1152]{1,0:T(8,128)(2,1)S(1)}, u32[]{:S(2)}, u32[]{:S(2)}) %collective-permute-start.8) | collective-permute-done | bytes 442400 | tf_op jit(solution)/shard_map/end_far/ppermute | solution.py:321
  47.2 0.0 collective-permute-done.6.refs_6_
  47.3 0.7 collective-permute-start.9
  47.9 0.4 collective-permute-done.7.refs_7_
  48.4 3.4 %collective-permute-start.10 = (bf16[192,1152]{1,0:T(8,128)(2,1)S(1)}, bf16[192,1152]{1,0:T(8,128)(2,1)S(1)}, u32[]{:S(2)}, u32[]{:S(2)}) collective-permute-start(bf16[192,1152]{1,0:T(8,128)(2,1)S(1)} %collective-permute-done.8.refs_9_), channel_id=1, source_target_pairs={{0,4},{4,0},{24,28},{28,24},{1,5},{5,1},{25,29},{29,25},{2,6},{6,2... | collective-permute-start | bytes 1327112 | tf_op jit(solution)/shard_map/end_far_across/ppermute | solution.py:327
  51.8 0.0 collective-permute-done.11.refs_9_.refs_13_
  51.8 0.0 copy-done.1
  51.8 7.9 %project_early.1 = (f32[768,1152]{1,0:T(8,128)S(1)}, f32[768,1152]{1,0:T(8,128)S(1)}) custom-call(bf16[192,1152]{1,0:T(8,128)(2,1)S(1)} %pad_maximum_fusion.refs_0_, bf16[192,1152]{1,0:T(8,128)(2,1)S(1)} %collective-permute-done.refs_1_, bf16[192,1152]{1,0:T(8,128)(2,1)S(1)} %collective-permute-done.1.refs_2_, ...), custom_call_target="tpu_custom_call" | custom-call | tf_op jit(solution)/shard_map/project_early/pallas_call | solution.py:238
  59.7 0.0 collective-permute-done.9.refs_10_
  59.7 1.6 %collective-permute-done.10.refs_11_ = bf16[192,1152]{1,0:T(8,128)(2,1)S(1)} collective-permute-done((bf16[192,1152]{1,0:T(8,128)(2,1)S(1)}, bf16[192,1152]{1,0:T(8,128)(2,1)S(1)}, u32[]{:S(2)}, u32[]{:S(2)}) %collective-permute-start.10) | collective-permute-done | bytes 442400 | tf_op jit(solution)/shard_map/end_far_across/ppermute | solution.py:327
  61.3 0.0 collective-permute-done.12.refs_14_
  61.3 1.3 %collective-permute-start.13 = (bf16[512,1536]{1,0:T(8,128)(2,1)S(1)}, bf16[512,1536]{1,0:T(8,128)(2,1)S(1)}, u32[]{:S(2)}, u32[]{:S(2)}) collective-permute-start(bf16[512,1536]{1,0:T(8,128)(2,1)S(1)} %collective-permute-done.12.refs_14_), channel_id=1, source_target_pairs={{1,0},{3,2},{5,4},{7,6},{9,8},{11,10},{13,12},{15,14},{17,16},{19,... | collective-permute-start | bytes 4718600 | tf_op jit(solution)/shard_map/halo_first/ppermute | solution.py:407
  62.6 0.0 copy-done.2
  62.6 0.0 copy-done.3
  62.6 0.0 copy-done.4
  62.7 7.6 %project_late_attend.1 = (bf16[768,384]{1,0:T(8,128)(2,1)S(1)}, bf16[768,384]{1,0:T(8,128)(2,1)S(1)}, bf16[2048,384]{1,0:T(8,128)(2,1)S(1)}, bf16[2048,384]{1,0:T(8,128)(2,1)S(1)}, bf16[1536,768]{1,0:T(8,128)(2,1)S(1)}) custom-call(s32[1,3]{1,0:T(1,128)S(1)} %copy-done.2, s32[1,12]{1,0:T(1,128)S(1)} %copy-done.3, s32[1,12]{1,0:T(1,128)S(1)} %copy-done.4, ...), custom_call_target="tpu_custom_call" | custom-call | tf_op jit(solution)/shard_map/project_late_attend/pallas_call | solution.py:280
  70.3 2.3 %collective-permute-start.14 = (bf16[768,384]{1,0:T(8,128)(2,1)S(1)}, bf16[768,384]{1,0:T(8,128)(2,1)S(1)}, u32[]{:S(2)}, u32[]{:S(2)}) collective-permute-start(bf16[768,384]{1,0:T(8,128)(2,1)S(1)} %get-tuple-element.36), channel_id=1, source_target_pairs={{0,1},{1,0},{2,3},{3,2},{4,5},{5,4},{6,7},{7,6},{8,9},{9,8},{10,11... | collective-permute-start | bytes 1769480 | tf_op jit(solution)/shard_map/swap/ppermute | solution.py:414
  72.6 0.0 collective-permute-done.13.halo_ref
  72.6 5.2 %attend_own.1 = bf16[768,384]{1,0:T(8,128)(2,1)S(1)} custom-call(s32[1,3]{1,0:T(1,128)S(1)} %copy-done.2, s32[1,12]{1,0:T(1,128)S(1)} %copy-done.3, s32[1,12]{1,0:T(1,128)S(1)} %copy-done.4, bf16[768,384]{1,0:T(8,128)(2,1)S(1)} %get-tuple-element.31.q_ref, bf16[2048,384]{1,0:T(8,128)(2,1)S(1)} %get-tuple-element.32.k_ref, ...), custom_call_target="tpu_custom_call" | custom-call | tf_op jit(solution)/shard_map/attend_own/pallas_call | solution.py:305
  77.7 0.0 collective-permute-done.14
  77.8 0.1 broadcast_select_fusion.1
  77.9 1.1 %maximum_bitcast_fusion = bf16[1,768,768]{2,1,0:T(8,128)(2,1)} fusion(bf16[768,384]{1,0:T(8,128)(2,1)S(1)} %get-tuple-element.38, bf16[768,384]{1,0:T(8,128)(2,1)S(1)} %get-tuple-element.37), kind=kLoop, calls=%fused_computation | loop fusion | flops 2359296 | bytes 2359296 | tf_op jit(solution)/shard_map/broadcast_in_dim | solution.py:418
  (1 shorter events, 0.0 us)
Async XLA Ops:
  1.4 8.1 %collective-permute-start.2 = (bf16[192,1152]{1,0:T(8,128)(2,1)S(1)}, bf16[192,1152]{1,0:T(8,128)(2,1)S(1)}, u32[]{:S(2)}, u32[]{:S(2)}) collective-permute-start(bf16[192,1152]{1,0:T(8,128)(2,1)S(1)} %pad_maximum_fusion.refs_0_), channel_id=1, source_target_pairs={{8,16},{12,20},{16,8},{20,12},{9,17},{13,21},{17,9},{21,13},{10,18... | collective-permute-start | bytes 1327112 | tf_op jit(solution)/shard_map/mid/ppermute | solution.py:321
  2.1 15.8 %collective-permute-start.1 = (bf16[192,1152]{1,0:T(8,128)(2,1)S(1)}, bf16[192,1152]{1,0:T(8,128)(2,1)S(1)}, u32[]{:S(2)}, u32[]{:S(2)}) collective-permute-start(bf16[192,1152]{1,0:T(8,128)(2,1)S(1)} %pad_maximum_fusion.refs_0_), channel_id=1, source_target_pairs={{8,0},{12,4},{16,24},{20,28},{0,8},{4,12},{24,16},{28,20},{9,1},{1... | collective-permute-start | bytes 1327112 | tf_op jit(solution)/shard_map/near/ppermute | solution.py:321
  7.9 11.3 %collective-permute-start = (bf16[192,1152]{1,0:T(8,128)(2,1)S(1)}, bf16[192,1152]{1,0:T(8,128)(2,1)S(1)}, u32[]{:S(2)}, u32[]{:S(2)}) collective-permute-start(bf16[192,1152]{1,0:T(8,128)(2,1)S(1)} %pad_maximum_fusion.refs_0_), channel_id=1, source_target_pairs={{0,4},{4,0},{8,12},{12,8},{16,20},{20,16},{24,28},{28,24},{1,5},{5... | collective-permute-start | bytes 1327112 | tf_op jit(solution)/shard_map/half_across/ppermute | solution.py:327
  9.5 42.3 %collective-permute-start.11 = (bf16[768,1536]{1,0:T(8,128)(2,1)}, bf16[768,1536]{1,0:T(8,128)(2,1)S(1)}, u32[]{:S(2)}, u32[]{:S(2)}) collective-permute-start(bf16[768,1536]{1,0:T(8,128)(2,1)} %bitcast.3), channel_id=1, source_target_pairs={{0,1},{1,0},{2,3},{3,2},{4,5},{5,4},{6,7},{7,6},{8,9},{9,8},{10,11... | collective-permute-start | bytes 7077896 | tf_op jit(solution)/shard_map/partner/ppermute | solution.py:389
  19.3 12.3 %collective-permute-start.4 = (bf16[192,1152]{1,0:T(8,128)(2,1)S(1)}, bf16[192,1152]{1,0:T(8,128)(2,1)S(1)}, u32[]{:S(2)}, u32[]{:S(2)}) collective-permute-start(bf16[192,1152]{1,0:T(8,128)(2,1)S(1)} %collective-permute-done.2.refs_4_), channel_id=1, source_target_pairs={{8,0},{12,4},{16,24},{20,28},{9,1},{13,5},{17,25},{21,29},{10,2},{... | collective-permute-start | bytes 1327112 | tf_op jit(solution)/shard_map/end_mid/ppermute | solution.py:321
  20.6 11.0 %collective-permute-start.5 = (bf16[192,1152]{1,0:T(8,128)(2,1)S(1)}, bf16[192,1152]{1,0:T(8,128)(2,1)S(1)}, u32[]{:S(2)}, u32[]{:S(2)}) collective-permute-start(bf16[192,1152]{1,0:T(8,128)(2,1)S(1)} %collective-permute-done.1.refs_2_), channel_id=1, source_target_pairs={{8,16},{12,20},{16,8},{20,12},{9,17},{13,21},{17,9},{21,13},{10,18... | collective-permute-start | bytes 1327112 | tf_op jit(solution)/shard_map/mid_far/ppermute | solution.py:321
  21.3 10.5 %collective-permute-start.3 = (bf16[192,1152]{1,0:T(8,128)(2,1)S(1)}, bf16[192,1152]{1,0:T(8,128)(2,1)S(1)}, u32[]{:S(2)}, u32[]{:S(2)}) collective-permute-start(bf16[192,1152]{1,0:T(8,128)(2,1)S(1)} %collective-permute-done.1.refs_2_), channel_id=1, source_target_pairs={{0,4},{4,0},{8,12},{12,8},{16,20},{20,16},{24,28},{28,24},{1,5},{5... | collective-permute-start | bytes 1327112 | tf_op jit(solution)/shard_map/near_across/ppermute | solution.py:327
  22.9 1.7 %copy-start = (bf16[1,768,1536]{2,1,0:T(8,128)(2,1)S(1)}, bf16[1,768,1536]{2,1,0:T(8,128)(2,1)}, u32[]{:S(2)}) copy-start(bf16[1,768,1536]{2,1,0:T(8,128)(2,1)} %param.5) | copy-start | bytes 7077892
  24.5 27.3 %copy-start.1 = (bf16[1,768,1536]{2,1,0:T(8,128)(2,1)S(1)}, bf16[1,768,1536]{2,1,0:T(8,128)(2,1)}, u32[]{:S(2)}) copy-start(bf16[1,768,1536]{2,1,0:T(8,128)(2,1)} %param.5) | copy-start | bytes 7077892
  24.7 38.0 %copy-start.2 = (s32[1,3]{1,0:T(1,128)S(1)}, s32[1,3]{1,0:T(1,128)}, u32[]{:S(2)}) copy-start(s32[1,3]{1,0:T(1,128)} %start_ref.3) | copy-start | bytes 40
  24.7 38.0 %copy-start.3 = (s32[1,12]{1,0:T(1,128)S(1)}, s32[1,12]{1,0:T(1,128)}, u32[]{:S(2)}) copy-start(s32[1,12]{1,0:T(1,128)} %owner_ref.3) | copy-start | bytes 148
  24.7 38.0 %copy-start.4 = (s32[1,12]{1,0:T(1,128)S(1)}, s32[1,12]{1,0:T(1,128)}, u32[]{:S(2)}) copy-start(s32[1,12]{1,0:T(1,128)} %left_ref.3) | copy-start | bytes 148
  31.8 29.6 %collective-permute-start.12 = (bf16[512,1536]{1,0:T(8,128)(2,1)S(1)}, bf16[512,1536]{1,0:T(8,128)(2,1)S(1)}, u32[]{:S(2)}, u32[]{:S(2)}) collective-permute-start(bf16[512,1536]{1,0:T(8,128)(2,1)S(1)} %take_tail.1), channel_id=1, source_target_pairs={{1,3},{5,7},{9,11},{13,15},{17,19},{21,23},{25,27},{29,31}} | collective-permute-start | bytes 4718600 | tf_op jit(solution)/shard_map/halo/ppermute | solution.py:400
  32.5 14.7 %collective-permute-start.8 = (bf16[192,1152]{1,0:T(8,128)(2,1)S(1)}, bf16[192,1152]{1,0:T(8,128)(2,1)S(1)}, u32[]{:S(2)}, u32[]{:S(2)}) collective-permute-start(bf16[192,1152]{1,0:T(8,128)(2,1)S(1)} %collective-permute-done.5.refs_8_), channel_id=1, source_target_pairs={{8,0},{12,4},{16,24},{20,28},{9,1},{13,5},{17,25},{21,29},{10,2},{... | collective-permute-start | bytes 1327112 | tf_op jit(solution)/shard_map/end_far/ppermute | solution.py:321
  33.8 13.4 %collective-permute-start.6 = (bf16[192,1152]{1,0:T(8,128)(2,1)S(1)}, bf16[192,1152]{1,0:T(8,128)(2,1)S(1)}, u32[]{:S(2)}, u32[]{:S(2)}) collective-permute-start(bf16[192,1152]{1,0:T(8,128)(2,1)S(1)} %collective-permute-done.2.refs_4_), channel_id=1, source_target_pairs={{8,12},{12,8},{16,20},{20,16},{9,13},{13,9},{17,21},{21,17},{10,14... | collective-permute-start | bytes 1327112 | tf_op jit(solution)/shard_map/mid_across/ppermute | solution.py:327
  34.5 13.8 %collective-permute-start.7 = (bf16[192,1152]{1,0:T(8,128)(2,1)S(1)}, bf16[192,1152]{1,0:T(8,128)(2,1)S(1)}, u32[]{:S(2)}, u32[]{:S(2)}) collective-permute-start(bf16[192,1152]{1,0:T(8,128)(2,1)S(1)} %collective-permute-done.4.refs_5_), channel_id=1, source_target_pairs={{0,4},{4,0},{24,28},{28,24},{1,5},{5,1},{25,29},{29,25},{2,6},{6,2... | collective-permute-start | bytes 1327112 | tf_op jit(solution)/shard_map/end_mid_across/ppermute | solution.py:327
  47.3 12.4 %collective-permute-start.9 = (bf16[192,1152]{1,0:T(8,128)(2,1)S(1)}, bf16[192,1152]{1,0:T(8,128)(2,1)S(1)}, u32[]{:S(2)}, u32[]{:S(2)}) collective-permute-start(bf16[192,1152]{1,0:T(8,128)(2,1)S(1)} %collective-permute-done.5.refs_8_), channel_id=1, source_target_pairs={{8,12},{12,8},{16,20},{20,16},{9,13},{13,9},{17,21},{21,17},{10,14... | collective-permute-start | bytes 1327112 | tf_op jit(solution)/shard_map/mid_far_across/ppermute | solution.py:327
  48.4 13.0 %collective-permute-start.10 = (bf16[192,1152]{1,0:T(8,128)(2,1)S(1)}, bf16[192,1152]{1,0:T(8,128)(2,1)S(1)}, u32[]{:S(2)}, u32[]{:S(2)}) collective-permute-start(bf16[192,1152]{1,0:T(8,128)(2,1)S(1)} %collective-permute-done.8.refs_9_), channel_id=1, source_target_pairs={{0,4},{4,0},{24,28},{28,24},{1,5},{5,1},{25,29},{29,25},{2,6},{6,2... | collective-permute-start | bytes 1327112 | tf_op jit(solution)/shard_map/end_far_across/ppermute | solution.py:327
  61.3 11.2 %collective-permute-start.13 = (bf16[512,1536]{1,0:T(8,128)(2,1)S(1)}, bf16[512,1536]{1,0:T(8,128)(2,1)S(1)}, u32[]{:S(2)}, u32[]{:S(2)}) collective-permute-start(bf16[512,1536]{1,0:T(8,128)(2,1)S(1)} %collective-permute-done.12.refs_14_), channel_id=1, source_target_pairs={{1,0},{3,2},{5,4},{7,6},{9,8},{11,10},{13,12},{15,14},{17,16},{19,... | collective-permute-start | bytes 4718600 | tf_op jit(solution)/shard_map/halo_first/ppermute | solution.py:407
  70.3 7.5 %collective-permute-start.14 = (bf16[768,384]{1,0:T(8,128)(2,1)S(1)}, bf16[768,384]{1,0:T(8,128)(2,1)S(1)}, u32[]{:S(2)}, u32[]{:S(2)}) collective-permute-start(bf16[768,384]{1,0:T(8,128)(2,1)S(1)} %get-tuple-element.36), channel_id=1, source_target_pairs={{0,1},{1,0},{2,3},{3,2},{4,5},{5,4},{6,7},{7,6},{8,9},{9,8},{10,11... | collective-permute-start | bytes 1769480 | tf_op jit(solution)/shard_map/swap/ppermute | solution.py:414
where the time goes:
time: 80.3 us; the launch traced here: 79 us
  waiting for transfers between devices  28.3 us (35%)
  starting transfers between devices  25.5 us (32%)
  Pallas kernels  20.8 us (26%)
  other arithmetic  2.57 us (3%)
  local copies, waits for them, and re-layouts  1.69 us (2%)
    ppermute x5, waiting for transfers between devices, along(): lax.ppermute(block, 'dp', [(2 * a + s, 2 * b + s) for a, b in hops for s...  24.6 us
    ppermute x6, starting transfers between devices, across(): lax.ppermute(block, 'dp', [(2 * a + s, 2 * a + 1 - s) for a in places for...  11.3 us
    ppermute x5, starting transfers between devices, along(): lax.ppermute(block, 'dp', [(2 * a + s, 2 * b + s) for a, b in hops for s...  9.84 us
    pallas_call x1, Pallas kernels, project_early(): pl.pallas_call(functools.partial(early_kernel, blocks), out_shape=[jax.Sh...  7.87 us
    pallas_call x1, Pallas kernels, project_late_attend(): pl.pallas_call(functools.partial(late_kernel, blocks), out_shape=[queries...  7.63 us
    pallas_call x1, Pallas kernels, attend_own(): pl.pallas_call(own_kernel, out_shape=jax.ShapeDtypeStruct((rows, width),...  5.18 us
    ppermute x6, waiting for transfers between devices, across(): lax.ppermute(block, 'dp', [(2 * a + s, 2 * a + 1 - s) for a in places for...  3.69 us
    ppermute x1, starting transfers between devices, local(): lax.ppermute(partner_out, 'tm', [(i, i ^ 1) for i in range(members)])  2.27 us
  transfers between devices with their start and end apart: 15, of which 7 were waited for; matrix products, arithmetic and copies ran while one was open for 0% of the time, Pallas kernels for 26%

commit v1 on v0

--- a/solution.py
+++ b/solution.py
@@ -85,7 +85,7 @@
 def late_kernel(blocks, start_ref, owner_ref, left_ref, *refs):
     n = len(blocks.operands)
     own_ref, partner_ref, halo_ref, own_sum, partner_sum = refs[n : n + 5]
-    out_ref, q_own, k_out, v_out, kv_out, q_partner, w_s, own_s, partner_s, sems = refs[n + 5 :]
+    out_ref, q_out, k_out, v_out, kv_out, w_s, own_s, partner_s, sems = refs[n + 5 :]
     depth = w_s.shape[0]
     width = w_s.shape[1] // 3
     rows = own_s.shape[0]
@@ -101,18 +101,12 @@
     copies = start_all(sems, pairs)
     for copy in copies[:n_first]:
         copy.wait()
-    for x_s, acc, query, place in (
-        (partner_s, partner_sum, q_partner, 1 - core),
-        (own_s, own_sum, q_own, core),
-    ):
-        row = pl.multiple_of(place * rows + REACH, STRETCH)
-        for third, dst in enumerate((query, k_out, v_out)):
+    for x_s, acc, place in ((partner_s, partner_sum, 1 - core), (own_s, own_sum, core)):
+        row = pl.multiple_of(place * rows, STRETCH)
+        for third, (dst, skip) in enumerate(((q_out, 0), (k_out, REACH), (v_out, REACH))):
             cols = slice(third * width, (third + 1) * width)
             value = (acc[:, cols] + dot(x_s[...], w_s[:, cols])).astype(jnp.bfloat16)
-            if third == 0:
-                dst[...] = value
-            else:
-                dst[pl.ds(row, rows), :] = value
+            dst[pl.ds(pl.multiple_of(row + skip, STRETCH), rows), :] = value
     for copy in copies[n_first:]:
         copy.wait()
 
@@ -121,12 +115,17 @@
         k_out[:REACH, :] = dot(halo_ref[...], kv_out[:, :width]).astype(jnp.bfloat16)
         v_out[:REACH, :] = dot(halo_ref[...], kv_out[:, width:]).astype(jnp.bfloat16)
 
-    first = pl.multiple_of((1 - core) * rows, STRETCH)
-    attend(start_ref, owner_ref, left_ref, 1 - core, q_partner, 0, k_out, v_out, first, out_ref)
+    chunks = rows // STRETCH
+
+    def block_of(i):
+        return jnp.where(i < chunks, (1 - core) * chunks + i, i - chunks + LEFT)
+
+    count = jnp.where(core == 0, 2 * chunks - LEFT, chunks)
+    attend(start_ref, owner_ref, left_ref, q_out, k_out, v_out, 0, count, block_of, out_ref)
 
 
 def own_kernel(
-    start_ref, owner_ref, left_ref, q_ref, k_ref, v_ref, kv_ref, halo_ref, out_ref, k_s, v_s
+    start_ref, owner_ref, left_ref, q_ref, k_ref, v_ref, kv_ref, halo_ref, done_ref, out_ref, k_s, v_s
 ):
     rows, width = out_ref.shape
     core = lax.axis_index("tm") % 2
@@ -144,12 +143,23 @@
         k_s[:REACH, :] = k_ref[rows : rows + REACH, :]
         v_s[:REACH, :] = v_ref[rows : rows + REACH, :]
 
-    attend(start_ref, owner_ref, left_ref, core, q_ref, 0, k_s, v_s, 0, out_ref)
-
-
-def attend(start_ref, owner_ref, left_ref, place, q_s, q_first, k_s, v_s, k_first, out_ref):
-    rows, width = out_ref.shape
     chunks = rows // STRETCH
+    base = core * chunks
+    count = jnp.where(core == 0, LEFT, chunks)
+
+    def block_of(i):
+        return base + i
+
+    attend(start_ref, owner_ref, left_ref, q_ref, k_s, v_s, base, count, block_of, out_ref)
+
+    @pl.when(core == 0)
+    def _():
+        out_ref[REACH:, :] = done_ref[rows : 2 * rows - REACH, :]
+
+
+def attend(start_ref, owner_ref, left_ref, q_s, k_s, v_s, k_base, count, block_of, out_ref):
+    width = out_ref.shape[1]
+    chunks = q_s.shape[0] // STRETCH
     pair = lax.axis_index("tm") // 2
     lane = lax.broadcasted_iota(jnp.int32, (1, width), 1)
     heads = width // HEAD_DIM
@@ -205,10 +215,12 @@
             value = jnp.where(live, value, 0.0).astype(jnp.bfloat16)
             out_ref[pl.ds(out_row, STRETCH), tile * LANES : (tile + 1) * LANES] = value
 
-    @pl.loop(0, chunks)
+    @pl.loop(0, count)
     def _(i):
-        row = pl.multiple_of(i * STRETCH, STRETCH)
-        chunk = (pair * 2 + place) * chunks + i
+        block = block_of(i)
+        out_row = pl.multiple_of(i * STRETCH, STRETCH)
+        q_row = pl.multiple_of(block * STRETCH, STRETCH)
+        chunk = pair * chunks + block
         left = left_ref[0, chunk]
         start = start_ref[0, owner_ref[0, chunk]]
         lowest = jnp.maximum((chunk - left) * STRETCH, start)
@@ -216,9 +228,9 @@
 
             @pl.when(left == back)
             def _():
-                q_row = pl.multiple_of(q_first + row, STRETCH)
-                k_row = pl.multiple_of(k_first + row + (LEFT - back) * STRETCH, STRETCH)
-                attend_block(chunk, start, lowest, q_row, k_row, (back + 1) * STRETCH, out_ref, row)
+                k_row = pl.multiple_of((block - k_base + LEFT - back) * STRETCH, STRETCH)
+                span = (back + 1) * STRETCH
+                attend_block(chunk, start, lowest, q_row, k_row, span, out_ref, out_row)
 
 
 def after(value, *others):
@@ -276,12 +288,11 @@
     cols = blocks.operands[0].shape[1]
     width = cols // 3
     keys = jax.ShapeDtypeStruct((2 * rows + REACH, width), jnp.bfloat16)
-    queries = jax.ShapeDtypeStruct((rows, width), jnp.bfloat16)
     return pl.pallas_call(
         functools.partial(late_kernel, blocks),
         out_shape=[
-            queries,
-            queries,
+            jax.ShapeDtypeStruct((2 * rows - REACH, width), jnp.bfloat16),
+            jax.ShapeDtypeStruct((2 * rows, width), jnp.bfloat16),
             keys,
             keys,
             jax.ShapeDtypeStruct((depth, 2 * width), jnp.bfloat16),
@@ -289,7 +300,6 @@
         in_specs=[SMEM_SPEC] * 3 + [ANY_SPEC] * (len(blocks.operands) + 2) + [VMEM_SPEC] * 3,
         out_specs=[VMEM_SPEC] * 5,
         scratch_shapes=[
-            pltpu.VMEM((rows, width), jnp.bfloat16),
             pltpu.VMEM((late_depth, cols), jnp.bfloat16),
             pltpu.VMEM((rows, late_depth), jnp.bfloat16),
             pltpu.VMEM((rows, late_depth), jnp.bfloat16),
@@ -300,20 +310,21 @@
     )(*tables, *blocks.operands, inputs, partner, halo, *sums)
 
 
-def attend_own(tables, query, keys, values, weights, halo):
-    rows, width = query.shape
+def attend_own(tables, queries, keys, values, weights, halo, done):
+    rows, width = queries.shape
+    rows //= 2
     return pl.pallas_call(
         own_kernel,
         out_shape=jax.ShapeDtypeStruct((rows, width), jnp.bfloat16),
-        in_specs=[SMEM_SPEC] * 3 + [VMEM_SPEC] * 5,
+        in_specs=[SMEM_SPEC] * 3 + [VMEM_SPEC] * 6,
         out_specs=VMEM_SPEC,
         scratch_shapes=[pltpu.VMEM((rows + REACH, width), jnp.bfloat16)] * 2,
         compiler_params=pltpu.CompilerParams(vmem_limit_bytes=20 * MIB),
         name="attend_own",
-    )(*tables, query, keys, values, weights, halo)
-
-
-def gather_neighbours(half):
+    )(*tables, queries, keys, values, weights, halo, done)
+
+
+def gather_neighbours(half, tail):
     size = half.shape[0]
 
     def along(name, block, hops):
@@ -332,7 +343,7 @@
     outward = [(1, 0), (2, 3)]
     between = [(1, 2), (2, 1)]
     near = along("near", half, outward + [(0, 1), (3, 2)])
-    mid = along("mid", half, between)
+    mid = along("mid", after(half, tail), between)
     half_across = across("half_across", half, line)
     mid_far = along("mid_far", near, between)
     near_across = across("near_across", after(near, half_across, mid), line)
@@ -341,7 +352,7 @@
     end_mid_across = across("end_mid_across", after(end_mid, near_across), ends)
     end_far = along("end_far", after(mid_far, end_mid), outward)
     mid_far_across = across("mid_far_across", after(mid_far, mid_across, end_far), middles)
-    end_far_across = across("end_far_across", after(end_far, end_mid_across), ends)
+    end_far_across = across("end_far_across", after(end_far, near_across), ends)
 
     def find():
         index = lax.axis_index("dp")
@@ -388,7 +399,7 @@
     with jax.named_scope("partner"):
         partner = lax.ppermute(inputs, "tm", [(i, i ^ 1) for i in range(members)])
     if lax.axis_size("dp") == 8:
-        blocks, marks = gather_neighbours(half)
+        blocks, marks = gather_neighbours(half, tail)
     else:
         weights = lax.all_gather(half, "dp", axis=0, tiled=True)
         late_first = depth - depth // GROUPS
@@ -407,12 +418,13 @@
         halo_first = lax.ppermute(
             after(halo, *marks[2], *sums), "tm", [(i + 1, i) for i in range(0, members, 2)]
         )
-    partner_out, query, keys, values, weights = project_late_attend(
+    attended, queries, keys, values, weights = project_late_attend(
         tables, blocks, inputs, partner, halo, sums
     )
     with jax.named_scope("swap"):
-        other = lax.ppermute(partner_out, "tm", [(i, i ^ 1) for i in range(members)])
-    own_out = attend_own(tables, query, keys, values, weights, halo_first)
+        other = lax.ppermute(attended, "tm", [(i, i ^ 1) for i in range(members)])
+    own_out = attend_own(tables, queries, keys, values, weights, halo_first, attended)
+    other = other[: inputs.shape[0]]
     left = jnp.where(core == 0, own_out, other)
     right = jnp.where(core == 0, other, own_out)
     return jnp.concatenate([left, right], axis=1)[None]

time: 80.3 us -> 81.1 us (level); the launches traced: 79 us -> 80.8 us
  waiting for transfers between devices: 28.3 us -> 33.4 us
  starting transfers between devices: 25.5 us -> 22.1 us
    ppermute x6, waiting for transfers between devices: 3.69 us -> 10.7 us  [across(): lax.ppermute(block, 'dp', [(2 * a + s, 2 * a + 1 - s) for a in places for...]
    ppermute x5, starting transfers between devices: 9.84 us -> 7.16 us  [along(): lax.ppermute(block, 'dp', [(2 * a + s, 2 * b + s) for a, b in hops for s...]
    ppermute x5, waiting for transfers between devices: 24.6 us -> 22.7 us  [along(): lax.ppermute(block, 'dp', [(2 * a + s, 2 * b + s) for a, b in hops for s...]
  transfers between devices with their start and end apart: 15 -> 15, of which waited for: 7 -> 6; matrix products, arithmetic and copies ran while one was open for 0% -> 0% of each run, Pallas kernels for 26% -> 26%
where the time goes in v1:
time: 81.1 us; the launch traced here: 80.8 us
  waiting for transfers between devices  33.4 us (41%)
  starting transfers between devices  22.1 us (27%)
  Pallas kernels  20.8 us (26%)
  other arithmetic  2.57 us (3%)
  local copies, waits for them, and re-layouts  1.69 us (2%)
    ppermute x5, waiting for transfers between devices, along(): lax.ppermute(block, 'dp', [(2 * a + s, 2 * b + s) for a, b in hops for s...  22.7 us
    ppermute x6, starting transfers between devices, across(): lax.ppermute(block, 'dp', [(2 * a + s, 2 * a + 1 - s) for a in places for...  11.3 us
    ppermute x6, waiting for transfers between devices, across(): lax.ppermute(block, 'dp', [(2 * a + s, 2 * a + 1 - s) for a in places for...  10.7 us
    pallas_call x1, Pallas kernels, project_late_attend(): pl.pallas_call(functools.partial(late_kernel, blocks), out_shape=[jax.Sha...  8.42 us
    pallas_call x1, Pallas kernels, project_early(): pl.pallas_call(functools.partial(early_kernel, blocks), out_shape=[jax.Sh...  7.87 us
    ppermute x5, starting transfers between devices, along(): lax.ppermute(block, 'dp', [(2 * a + s, 2 * b + s) for a, b in hops for s...  7.16 us
    pallas_call x1, Pallas kernels, attend_own(): pl.pallas_call(own_kernel, out_shape=jax.ShapeDtypeStruct((rows, width),...  4.42 us
    unnamed x10, local copies, waits for them, and re-layouts  1.69 us
  transfers between devices with their start and end apart: 15, of which 6 were waited for; matrix products, arithmetic and copies ran while one was open for 0% of the time, Pallas kernels for 26%

profile of v1, /device:TPU:0, one launch (start us, length us, event | category | flops | bytes accessed | tf_op | source)
XLA Modules:
  0.0 80.8 jit_solution(12565194508023913883)
XLA Ops:
  0.0 1.3 %slice_select_fusion.2 = (bf16[192,384]{1,0:T(8,128)(2,1)S(1)}, bf16[192,384]{1,0:T(8,128)(2,1)S(1)}, bf16[192,384]{1,0:T(8,128)(2,1)S(1)}) fusion(bf16[192,2304]{1,0:T(8,128)(2,1)} %param.6, pred[]{:T(512)S(6)} %eq.4), kind=kLoop, calls=%fused_computation.6 | loop fusion | flops 221184 | bytes 1327105 | tf_op jit(solution)/shard_map/jit(_where)/select_n | solution.py:395
  1.4 3.1 %collective-permute-start.1 = (bf16[192,1152]{1,0:T(8,128)(2,1)S(1)}, bf16[192,1152]{1,0:T(8,128)(2,1)S(1)}, u32[]{:S(2)}, u32[]{:S(2)}) collective-permute-start(bf16[192,1152]{1,0:T(8,128)(2,1)S(1)} %pad_maximum_fusion.refs_0_), channel_id=1, source_target_pairs={{8,0},{12,4},{16,24},{20,28},{0,8},{4,12},{24,16},{28,20},{9,1},{1... | collective-permute-start | bytes 1327112 | tf_op jit(solution)/shard_map/near/ppermute | solution.py:332
  4.4 1.5 %collective-permute-start = (bf16[192,1152]{1,0:T(8,128)(2,1)S(1)}, bf16[192,1152]{1,0:T(8,128)(2,1)S(1)}, u32[]{:S(2)}, u32[]{:S(2)}) collective-permute-start(bf16[192,1152]{1,0:T(8,128)(2,1)S(1)} %pad_maximum_fusion.refs_0_), channel_id=1, source_target_pairs={{0,4},{4,0},{8,12},{12,8},{16,20},{20,16},{24,28},{28,24},{1,5},{5... | collective-permute-start | bytes 1327112 | tf_op jit(solution)/shard_map/half_across/ppermute | solution.py:338
  6.0 0.0 copy-start
  6.0 1.7 %copy-done = bf16[1,768,1536]{2,1,0:T(8,128)(2,1)S(1)} copy-done((bf16[1,768,1536]{2,1,0:T(8,128)(2,1)S(1)}, bf16[1,768,1536]{2,1,0:T(8,128)(2,1)}, u32[]{:S(2)}) %copy-start) | copy-done | bytes 2359320
  7.6 0.0 copy-start.1
  7.6 0.1 take_tail.1
  7.8 0.0 copy-start.2
  7.8 0.0 copy-start.3
  7.8 0.0 copy-start.4
  7.8 0.8 %collective-permute-start.2 = (bf16[192,1152]{1,0:T(8,128)(2,1)S(1)}, bf16[192,1152]{1,0:T(8,128)(2,1)S(1)}, u32[]{:S(2)}, u32[]{:S(2)}) collective-permute-start(bf16[192,1152]{1,0:T(8,128)(2,1)S(1)} %pad_maximum_fusion.refs_0_), channel_id=1, source_target_pairs={{8,16},{12,20},{16,8},{20,12},{9,17},{13,21},{17,9},{21,13},{10,18... | collective-permute-start | bytes 1327112 | tf_op jit(solution)/shard_map/mid/ppermute | solution.py:332
  8.6 0.1 collective-permute-start.11
  8.7 5.9 %collective-permute-done.1.refs_2_ = bf16[192,1152]{1,0:T(8,128)(2,1)S(1)} collective-permute-done((bf16[192,1152]{1,0:T(8,128)(2,1)S(1)}, bf16[192,1152]{1,0:T(8,128)(2,1)S(1)}, u32[]{:S(2)}, u32[]{:S(2)}) %collective-permute-start.1) | collective-permute-done | bytes 442400 | tf_op jit(solution)/shard_map/near/ppermute | solution.py:332
  14.6 1.5 %collective-permute-done.refs_1_ = bf16[192,1152]{1,0:T(8,128)(2,1)S(1)} collective-permute-done((bf16[192,1152]{1,0:T(8,128)(2,1)S(1)}, bf16[192,1152]{1,0:T(8,128)(2,1)S(1)}, u32[]{:S(2)}, u32[]{:S(2)}) %collective-permute-start) | collective-permute-done | bytes 442400 | tf_op jit(solution)/shard_map/half_across/ppermute | solution.py:338
  16.1 0.0 collective-permute-done.2.refs_4_
  16.1 0.7 collective-permute-start.5
  16.8 1.6 %collective-permute-start.3 = (bf16[192,1152]{1,0:T(8,128)(2,1)S(1)}, bf16[192,1152]{1,0:T(8,128)(2,1)S(1)}, u32[]{:S(2)}, u32[]{:S(2)}) collective-permute-start(bf16[192,1152]{1,0:T(8,128)(2,1)S(1)} %collective-permute-done.1.refs_2_), channel_id=1, source_target_pairs={{0,4},{4,0},{8,12},{12,8},{16,20},{20,16},{24,28},{28,24},{1,5},{5... | collective-permute-start | bytes 1327112 | tf_op jit(solution)/shard_map/near_across/ppermute | solution.py:338
  18.4 1.3 %collective-permute-start.4 = (bf16[192,1152]{1,0:T(8,128)(2,1)S(1)}, bf16[192,1152]{1,0:T(8,128)(2,1)S(1)}, u32[]{:S(2)}, u32[]{:S(2)}) collective-permute-start(bf16[192,1152]{1,0:T(8,128)(2,1)S(1)} %collective-permute-done.2.refs_4_), channel_id=1, source_target_pairs={{8,0},{12,4},{16,24},{20,28},{9,1},{13,5},{17,25},{21,29},{10,2},{... | collective-permute-start | bytes 1327112 | tf_op jit(solution)/shard_map/end_mid/ppermute | solution.py:332
  19.6 0.0 collective-permute-done.5.refs_8_
  19.6 7.9 %collective-permute-done.3.refs_3_ = bf16[192,1152]{1,0:T(8,128)(2,1)S(1)} collective-permute-done((bf16[192,1152]{1,0:T(8,128)(2,1)S(1)}, bf16[192,1152]{1,0:T(8,128)(2,1)S(1)}, u32[]{:S(2)}, u32[]{:S(2)}) %collective-permute-start.3) | collective-permute-done | bytes 442400 | tf_op jit(solution)/shard_map/near_across/ppermute | solution.py:338
  27.6 8.6 %collective-permute-done.4.refs_5_ = bf16[192,1152]{1,0:T(8,128)(2,1)S(1)} collective-permute-done((bf16[192,1152]{1,0:T(8,128)(2,1)S(1)}, bf16[192,1152]{1,0:T(8,128)(2,1)S(1)}, u32[]{:S(2)}, u32[]{:S(2)}) %collective-permute-start.4) | collective-permute-done | bytes 442400 | tf_op jit(solution)/shard_map/end_mid/ppermute | solution.py:332
  36.2 0.8 collective-permute-start.12
  36.9 1.3 %collective-permute-start.8 = (bf16[192,1152]{1,0:T(8,128)(2,1)S(1)}, bf16[192,1152]{1,0:T(8,128)(2,1)S(1)}, u32[]{:S(2)}, u32[]{:S(2)}) collective-permute-start(bf16[192,1152]{1,0:T(8,128)(2,1)S(1)} %collective-permute-done.5.refs_8_), channel_id=1, source_target_pairs={{8,0},{12,4},{16,24},{20,28},{9,1},{13,5},{17,25},{21,29},{10,2},{... | collective-permute-start | bytes 1327112 | tf_op jit(solution)/shard_map/end_far/ppermute | solution.py:332
  38.2 0.7 collective-permute-start.6
  38.9 3.4 %collective-permute-start.7 = (bf16[192,1152]{1,0:T(8,128)(2,1)S(1)}, bf16[192,1152]{1,0:T(8,128)(2,1)S(1)}, u32[]{:S(2)}, u32[]{:S(2)}) collective-permute-start(bf16[192,1152]{1,0:T(8,128)(2,1)S(1)} %collective-permute-done.4.refs_5_), channel_id=1, source_target_pairs={{0,4},{4,0},{24,28},{28,24},{1,5},{5,1},{25,29},{29,25},{2,6},{6,2... | collective-permute-start | bytes 1327112 | tf_op jit(solution)/shard_map/end_mid_across/ppermute | solution.py:338
  42.4 8.1 %collective-permute-done.8.refs_9_ = bf16[192,1152]{1,0:T(8,128)(2,1)S(1)} collective-permute-done((bf16[192,1152]{1,0:T(8,128)(2,1)S(1)}, bf16[192,1152]{1,0:T(8,128)(2,1)S(1)}, u32[]{:S(2)}, u32[]{:S(2)}) %collective-permute-start.8) | collective-permute-done | bytes 442400 | tf_op jit(solution)/shard_map/end_far/ppermute | solution.py:332
  50.5 0.0 collective-permute-done.6.refs_6_
  50.5 0.7 collective-permute-start.9
  51.2 3.4 %collective-permute-start.10 = (bf16[192,1152]{1,0:T(8,128)(2,1)S(1)}, bf16[192,1152]{1,0:T(8,128)(2,1)S(1)}, u32[]{:S(2)}, u32[]{:S(2)}) collective-permute-start(bf16[192,1152]{1,0:T(8,128)(2,1)S(1)} %collective-permute-done.8.refs_9_), channel_id=1, source_target_pairs={{0,4},{4,0},{24,28},{28,24},{1,5},{5,1},{25,29},{29,25},{2,6},{6,2... | collective-permute-start | bytes 1327112 | tf_op jit(solution)/shard_map/end_far_across/ppermute | solution.py:338
  54.6 0.0 collective-permute-done.7.refs_7_
  54.6 0.0 collective-permute-done.11.refs_9_.refs_13_
  54.7 0.0 copy-done.1
  54.7 7.9 %project_early.1 = (f32[768,1152]{1,0:T(8,128)S(1)}, f32[768,1152]{1,0:T(8,128)S(1)}) custom-call(bf16[192,1152]{1,0:T(8,128)(2,1)S(1)} %pad_maximum_fusion.refs_0_, bf16[192,1152]{1,0:T(8,128)(2,1)S(1)} %collective-permute-done.refs_1_, bf16[192,1152]{1,0:T(8,128)(2,1)S(1)} %collective-permute-done.1.refs_2_, ...), custom_call_target="tpu_custom_call" | custom-call | tf_op jit(solution)/shard_map/project_early/pallas_call | solution.py:250
  62.5 0.0 collective-permute-done.9.refs_10_
  62.6 1.3 %collective-permute-done.10.refs_11_ = bf16[192,1152]{1,0:T(8,128)(2,1)S(1)} collective-permute-done((bf16[192,1152]{1,0:T(8,128)(2,1)S(1)}, bf16[192,1152]{1,0:T(8,128)(2,1)S(1)}, u32[]{:S(2)}, u32[]{:S(2)}) %collective-permute-start.10) | collective-permute-done | bytes 442400 | tf_op jit(solution)/shard_map/end_far_across/ppermute | solution.py:338
  63.9 0.0 collective-permute-done.12.refs_14_
  63.9 1.3 %collective-permute-start.13 = (bf16[512,1536]{1,0:T(8,128)(2,1)S(1)}, bf16[512,1536]{1,0:T(8,128)(2,1)S(1)}, u32[]{:S(2)}, u32[]{:S(2)}) collective-permute-start(bf16[512,1536]{1,0:T(8,128)(2,1)S(1)} %collective-permute-done.12.refs_14_), channel_id=1, source_target_pairs={{1,0},{3,2},{5,4},{7,6},{9,8},{11,10},{13,12},{15,14},{17,16},{19,... | collective-permute-start | bytes 4718600 | tf_op jit(solution)/shard_map/halo_first/ppermute | solution.py:418
  65.2 0.0 copy-done.2
  65.2 0.0 copy-done.3
  65.2 0.0 copy-done.4
  65.2 8.4 %project_late_attend.1 = (bf16[1024,384]{1,0:T(8,128)(2,1)S(1)}, bf16[1536,384]{1,0:T(8,128)(2,1)S(1)}, bf16[2048,384]{1,0:T(8,128)(2,1)S(1)}, bf16[2048,384]{1,0:T(8,128)(2,1)S(1)}, bf16[1536,768]{1,0:T(8,128)(2,1)S(1)}) custom-call(s32[1,3]{1,0:T(1,128)S(1)} %copy-done.2, s32[1,12]{1,0:T(1,128)S(1)} %copy-done.3, s32[1,12]{1,0:T(1,128)S(1)} %copy-done.4, ...), custom_call_target="tpu_custom_call" | custom-call | tf_op jit(solution)/shard_map/project_late_attend/pallas_call | solution.py:291
  73.6 1.5 %collective-permute-start.14 = (bf16[1024,384]{1,0:T(8,128)(2,1)S(1)}, bf16[1024,384]{1,0:T(8,128)(2,1)S(1)}, u32[]{:S(2)}, u32[]{:S(2)}) collective-permute-start(bf16[1024,384]{1,0:T(8,128)(2,1)S(1)} %get-tuple-element.38.done_ref), channel_id=1, source_target_pairs={{0,1},{1,0},{2,3},{3,2},{4,5},{5,4},{6,7},{7,6},{8,9},{9,8},{10,11... | collective-permute-start | bytes 2359304 | tf_op jit(solution)/shard_map/swap/ppermute | solution.py:425
  75.1 0.0 collective-permute-done.13.halo_ref
  75.1 4.4 %attend_own.1 = bf16[768,384]{1,0:T(8,128)(2,1)S(1)} custom-call(s32[1,3]{1,0:T(1,128)S(1)} %copy-done.2, s32[1,12]{1,0:T(1,128)S(1)} %copy-done.3, s32[1,12]{1,0:T(1,128)S(1)} %copy-done.4, bf16[1536,384]{1,0:T(8,128)(2,1)S(1)} %get-tuple-element.33.q_ref, bf16[2048,384]{1,0:T(8,128)(2,1)S(1)} %get-tuple-element.34.k_ref, ...), custom_call_target="tpu_custom_call" | custom-call | tf_op jit(solution)/shard_map/attend_own/pallas_call | solution.py:316
  79.5 0.0 collective-permute-done.14
  79.5 0.1 broadcast_select_fusion.1
  79.6 1.1 %maximum_bitcast_fusion = bf16[1,768,768]{2,1,0:T(8,128)(2,1)} fusion(bf16[768,384]{1,0:T(8,128)(2,1)S(1)} %get-tuple-element.40, bf16[768,384]{1,0:T(8,128)(2,1)S(1)} %get-tuple-element.39), kind=kLoop, calls=%fused_computation | loop fusion | flops 2359296 | bytes 2359296 | tf_op jit(solution)/shard_map/broadcast_in_dim | solution.py:430
  (1 shorter events, 0.0 us)
Async XLA Ops:
  1.4 13.3 %collective-permute-start.1 = (bf16[192,1152]{1,0:T(8,128)(2,1)S(1)}, bf16[192,1152]{1,0:T(8,128)(2,1)S(1)}, u32[]{:S(2)}, u32[]{:S(2)}) collective-permute-start(bf16[192,1152]{1,0:T(8,128)(2,1)S(1)} %pad_maximum_fusion.refs_0_), channel_id=1, source_target_pairs={{8,0},{12,4},{16,24},{20,28},{0,8},{4,12},{24,16},{28,20},{9,1},{1... | collective-permute-start | bytes 1327112 | tf_op jit(solution)/shard_map/near/ppermute | solution.py:332
  4.4 11.6 %collective-permute-start = (bf16[192,1152]{1,0:T(8,128)(2,1)S(1)}, bf16[192,1152]{1,0:T(8,128)(2,1)S(1)}, u32[]{:S(2)}, u32[]{:S(2)}) collective-permute-start(bf16[192,1152]{1,0:T(8,128)(2,1)S(1)} %pad_maximum_fusion.refs_0_), channel_id=1, source_target_pairs={{0,4},{4,0},{8,12},{12,8},{16,20},{20,16},{24,28},{28,24},{1,5},{5... | collective-permute-start | bytes 1327112 | tf_op jit(solution)/shard_map/half_across/ppermute | solution.py:338
  6.0 1.7 %copy-start = (bf16[1,768,1536]{2,1,0:T(8,128)(2,1)S(1)}, bf16[1,768,1536]{2,1,0:T(8,128)(2,1)}, u32[]{:S(2)}) copy-start(bf16[1,768,1536]{2,1,0:T(8,128)(2,1)} %param.5) | copy-start | bytes 7077892
  7.6 47.0 %copy-start.1 = (bf16[1,768,1536]{2,1,0:T(8,128)(2,1)S(1)}, bf16[1,768,1536]{2,1,0:T(8,128)(2,1)}, u32[]{:S(2)}) copy-start(bf16[1,768,1536]{2,1,0:T(8,128)(2,1)} %param.5) | copy-start | bytes 7077892
  7.8 57.4 %copy-start.2 = (s32[1,3]{1,0:T(1,128)S(1)}, s32[1,3]{1,0:T(1,128)}, u32[]{:S(2)}) copy-start(s32[1,3]{1,0:T(1,128)} %start_ref.3) | copy-start | bytes 40
  7.8 57.4 %copy-start.3 = (s32[1,12]{1,0:T(1,128)S(1)}, s32[1,12]{1,0:T(1,128)}, u32[]{:S(2)}) copy-start(s32[1,12]{1,0:T(1,128)} %owner_ref.3) | copy-start | bytes 148
  7.8 57.4 %copy-start.4 = (s32[1,12]{1,0:T(1,128)S(1)}, s32[1,12]{1,0:T(1,128)}, u32[]{:S(2)}) copy-start(s32[1,12]{1,0:T(1,128)} %left_ref.3) | copy-start | bytes 148
  7.8 8.3 %collective-permute-start.2 = (bf16[192,1152]{1,0:T(8,128)(2,1)S(1)}, bf16[192,1152]{1,0:T(8,128)(2,1)S(1)}, u32[]{:S(2)}, u32[]{:S(2)}) collective-permute-start(bf16[192,1152]{1,0:T(8,128)(2,1)S(1)} %pad_maximum_fusion.refs_0_), channel_id=1, source_target_pairs={{8,16},{12,20},{16,8},{20,12},{9,17},{13,21},{17,9},{21,13},{10,18... | collective-permute-start | bytes 1327112 | tf_op jit(solution)/shard_map/mid/ppermute | solution.py:332
  8.6 46.0 %collective-permute-start.11 = (bf16[768,1536]{1,0:T(8,128)(2,1)S(1)}, bf16[768,1536]{1,0:T(8,128)(2,1)S(1)}, u32[]{:S(2)}, u32[]{:S(2)}) collective-permute-start(bf16[768,1536]{1,0:T(8,128)(2,1)S(1)} %bitcast.4), channel_id=1, source_target_pairs={{0,1},{1,0},{2,3},{3,2},{4,5},{5,4},{6,7},{7,6},{8,9},{9,8},{10,11... | collective-permute-start | bytes 7077896 | tf_op jit(solution)/shard_map/partner/ppermute | solution.py:400
  16.1 3.6 %collective-permute-start.5 = (bf16[192,1152]{1,0:T(8,128)(2,1)S(1)}, bf16[192,1152]{1,0:T(8,128)(2,1)S(1)}, u32[]{:S(2)}, u32[]{:S(2)}) collective-permute-start(bf16[192,1152]{1,0:T(8,128)(2,1)S(1)} %collective-permute-done.1.refs_2_), channel_id=1, source_target_pairs={{8,16},{12,20},{16,8},{20,12},{9,17},{13,21},{17,9},{21,13},{10,18... | collective-permute-start | bytes 1327112 | tf_op jit(solution)/shard_map/mid_far/ppermute | solution.py:332
  16.8 10.8 %collective-permute-start.3 = (bf16[192,1152]{1,0:T(8,128)(2,1)S(1)}, bf16[192,1152]{1,0:T(8,128)(2,1)S(1)}, u32[]{:S(2)}, u32[]{:S(2)}) collective-permute-start(bf16[192,1152]{1,0:T(8,128)(2,1)S(1)} %collective-permute-done.1.refs_2_), channel_id=1, source_target_pairs={{0,4},{4,0},{8,12},{12,8},{16,20},{20,16},{24,28},{28,24},{1,5},{5... | collective-permute-start | bytes 1327112 | tf_op jit(solution)/shard_map/near_across/ppermute | solution.py:338
  18.4 17.8 %collective-permute-start.4 = (bf16[192,1152]{1,0:T(8,128)(2,1)S(1)}, bf16[192,1152]{1,0:T(8,128)(2,1)S(1)}, u32[]{:S(2)}, u32[]{:S(2)}) collective-permute-start(bf16[192,1152]{1,0:T(8,128)(2,1)S(1)} %collective-permute-done.2.refs_4_), channel_id=1, source_target_pairs={{8,0},{12,4},{16,24},{20,28},{9,1},{13,5},{17,25},{21,29},{10,2},{... | collective-permute-start | bytes 1327112 | tf_op jit(solution)/shard_map/end_mid/ppermute | solution.py:332
  36.2 27.7 %collective-permute-start.12 = (bf16[512,1536]{1,0:T(8,128)(2,1)S(1)}, bf16[512,1536]{1,0:T(8,128)(2,1)S(1)}, u32[]{:S(2)}, u32[]{:S(2)}) collective-permute-start(bf16[512,1536]{1,0:T(8,128)(2,1)S(1)} %take_tail.1), channel_id=1, source_target_pairs={{1,3},{5,7},{9,11},{13,15},{17,19},{21,23},{25,27},{29,31}} | collective-permute-start | bytes 4718600 | tf_op jit(solution)/shard_map/halo/ppermute | solution.py:411
  36.9 13.6 %collective-permute-start.8 = (bf16[192,1152]{1,0:T(8,128)(2,1)S(1)}, bf16[192,1152]{1,0:T(8,128)(2,1)S(1)}, u32[]{:S(2)}, u32[]{:S(2)}) collective-permute-start(bf16[192,1152]{1,0:T(8,128)(2,1)S(1)} %collective-permute-done.5.refs_8_), channel_id=1, source_target_pairs={{8,0},{12,4},{16,24},{20,28},{9,1},{13,5},{17,25},{21,29},{10,2},{... | collective-permute-start | bytes 1327112 | tf_op jit(solution)/shard_map/end_far/ppermute | solution.py:332
  38.2 12.3 %collective-permute-start.6 = (bf16[192,1152]{1,0:T(8,128)(2,1)S(1)}, bf16[192,1152]{1,0:T(8,128)(2,1)S(1)}, u32[]{:S(2)}, u32[]{:S(2)}) collective-permute-start(bf16[192,1152]{1,0:T(8,128)(2,1)S(1)} %collective-permute-done.2.refs_4_), channel_id=1, source_target_pairs={{8,12},{12,8},{16,20},{20,16},{9,13},{13,9},{17,21},{21,17},{10,14... | collective-permute-start | bytes 1327112 | tf_op jit(solution)/shard_map/mid_across/ppermute | solution.py:338
  38.9 15.7 %collective-permute-start.7 = (bf16[192,1152]{1,0:T(8,128)(2,1)S(1)}, bf16[192,1152]{1,0:T(8,128)(2,1)S(1)}, u32[]{:S(2)}, u32[]{:S(2)}) collective-permute-start(bf16[192,1152]{1,0:T(8,128)(2,1)S(1)} %collective-permute-done.4.refs_5_), channel_id=1, source_target_pairs={{0,4},{4,0},{24,28},{28,24},{1,5},{5,1},{25,29},{29,25},{2,6},{6,2... | collective-permute-start | bytes 1327112 | tf_op jit(solution)/shard_map/end_mid_across/ppermute | solution.py:338
  50.5 12.0 %collective-permute-start.9 = (bf16[192,1152]{1,0:T(8,128)(2,1)S(1)}, bf16[192,1152]{1,0:T(8,128)(2,1)S(1)}, u32[]{:S(2)}, u32[]{:S(2)}) collective-permute-start(bf16[192,1152]{1,0:T(8,128)(2,1)S(1)} %collective-permute-done.5.refs_8_), channel_id=1, source_target_pairs={{8,12},{12,8},{16,20},{20,16},{9,13},{13,9},{17,21},{21,17},{10,14... | collective-permute-start | bytes 1327112 | tf_op jit(solution)/shard_map/mid_far_across/ppermute | solution.py:338
  51.2 12.7 %collective-permute-start.10 = (bf16[192,1152]{1,0:T(8,128)(2,1)S(1)}, bf16[192,1152]{1,0:T(8,128)(2,1)S(1)}, u32[]{:S(2)}, u32[]{:S(2)}) collective-permute-start(bf16[192,1152]{1,0:T(8,128)(2,1)S(1)} %collective-permute-done.8.refs_9_), channel_id=1, source_target_pairs={{0,4},{4,0},{24,28},{28,24},{1,5},{5,1},{25,29},{29,25},{2,6},{6,2... | collective-permute-start | bytes 1327112 | tf_op jit(solution)/shard_map/end_far_across/ppermute | solution.py:338
  63.9 11.2 %collective-permute-start.13 = (bf16[512,1536]{1,0:T(8,128)(2,1)S(1)}, bf16[512,1536]{1,0:T(8,128)(2,1)S(1)}, u32[]{:S(2)}, u32[]{:S(2)}) collective-permute-start(bf16[512,1536]{1,0:T(8,128)(2,1)S(1)} %collective-permute-done.12.refs_14_), channel_id=1, source_target_pairs={{1,0},{3,2},{5,4},{7,6},{9,8},{11,10},{13,12},{15,14},{17,16},{19,... | collective-permute-start | bytes 4718600 | tf_op jit(solution)/shard_map/halo_first/ppermute | solution.py:418
  73.6 5.9 %collective-permute-start.14 = (bf16[1024,384]{1,0:T(8,128)(2,1)S(1)}, bf16[1024,384]{1,0:T(8,128)(2,1)S(1)}, u32[]{:S(2)}, u32[]{:S(2)}) collective-permute-start(bf16[1024,384]{1,0:T(8,128)(2,1)S(1)} %get-tuple-element.38.done_ref), channel_id=1, source_target_pairs={{0,1},{1,0},{2,3},{3,2},{4,5},{5,4},{6,7},{7,6},{8,9},{9,8},{10,11... | collective-permute-start | bytes 2359304 | tf_op jit(solution)/shard_map/swap/ppermute | solution.py:425

commit v2 on v0

--- a/solution.py
+++ b/solution.py
@@ -313,6 +313,28 @@
     )(*tables, query, keys, values, weights, halo)
 
 
+def at_end():
+    place = lax.axis_index("dp") // 2
+    return jnp.where((place == 0) | (place == 3), 1, 0)
+
+
+def choose_kernel(between_ref, end_ref, out_ref, sems):
+    for copy in start_all(sems, [((between_ref, end_ref), at_end(), out_ref)]):
+        copy.wait()
+
+
+def choose(between, end):
+    return pl.pallas_call(
+        choose_kernel,
+        out_shape=jax.ShapeDtypeStruct(end.shape, end.dtype),
+        in_specs=[ANY_SPEC] * 2,
+        out_specs=VMEM_SPEC,
+        scratch_shapes=[pltpu.SemaphoreType.DMA((1,))],
+        compiler_params=pltpu.CompilerParams(vmem_limit_bytes=2 * MIB),
+        name="choose",
+    )(between, end)
+
+
 def gather_neighbours(half):
     size = half.shape[0]
 
@@ -328,7 +350,7 @@
                 block, "dp", [(2 * a + s, 2 * a + 1 - s) for a in places for s in range(2)]
             )
 
-    line, ends, middles = range(4), (0, 3), (1, 2)
+    line = range(4)
     outward = [(1, 0), (2, 3)]
     between = [(1, 2), (2, 1)]
     near = along("near", half, outward + [(0, 1), (3, 2)])
@@ -337,16 +359,16 @@
     mid_far = along("mid_far", near, between)
     near_across = across("near_across", after(near, half_across, mid), line)
     end_mid = along("end_mid", mid, outward)
-    mid_across = across("mid_across", after(mid, near_across, mid_far), middles)
-    end_mid_across = across("end_mid_across", after(end_mid, near_across), ends)
     end_far = along("end_far", after(mid_far, end_mid), outward)
-    mid_far_across = across("mid_far_across", after(mid_far, mid_across, end_far), middles)
-    end_far_across = across("end_far_across", after(end_far, end_mid_across), ends)
+    second = choose(mid, end_mid)
+    second_across = across("second_across", after(second, near_across), line)
+    third = choose(mid_far, end_far)
+    third_across = across("third_across", after(third, second_across), line)
 
     def find():
         index = lax.axis_index("dp")
         place, side = index // 2, index % 2
-        is_end = jnp.where((place == 0) | (place == 3), 1, 0)
+        is_end = at_end()
         second = jnp.where(is_end == 1, place ^ 2, 3 - place)
         third = jnp.where(is_end == 1, 3 - place, place ^ 2)
         spots = (place, place ^ 1, second, third)
@@ -358,16 +380,12 @@
         (half_across,),
         (near,),
         (near_across,),
-        (mid, end_mid),
-        (mid_across, end_mid_across),
-        (mid_far, end_far),
-        (mid_far_across, end_far_across),
+        (second,),
+        (second_across,),
+        (third,),
+        (third_across,),
     ]
-    marks = (
-        (near_across, mid_far, end_mid),
-        (mid_across, end_mid_across, end_far),
-        (mid_far_across, end_far_across),
-    )
+    marks = (near_across, mid_far, end_mid), (second_across, end_far), (third_across,)
     return Blocks(blocks, 2, find), marks
 
 

time: 80.3 us -> 76.3 us (0.950); the launches traced: 79 us -> 76 us
  starting transfers between devices: 25.5 us -> 20.8 us
  waiting for transfers between devices: 28.3 us -> 29.9 us
    ppermute x6 -> x4, starting transfers between devices: 11.3 us -> 6.27 us  [across(): lax.ppermute(block, 'dp', [(2 * a + s, 2 * a + 1 - s) for a in places for...]
    ppermute x5, waiting for transfers between devices: 24.6 us -> 26.9 us  [along(): lax.ppermute(block, 'dp', [(2 * a + s, 2 * b + s) for a, b in hops for s...]
    ppermute x6 -> x4, waiting for transfers between devices: 3.69 us -> 3.07 us  [across(): lax.ppermute(block, 'dp', [(2 * a + s, 2 * a + 1 - s) for a in places for...]
  transfers between devices with their start and end apart: 15 -> 13, of which waited for: 7 -> 6; matrix products, arithmetic and copies ran while one was open for 0% -> 0% of each run, Pallas kernels for 26% -> 27%
where the time goes in v2:
time: 76.3 us; the launch traced here: 76 us
  waiting for transfers between devices  29.9 us (39%)
  Pallas kernels  20.9 us (27%)
  starting transfers between devices  20.8 us (27%)
  other arithmetic  2.57 us (3%)
  local copies, waits for them, and re-layouts  1.69 us (2%)
    ppermute x5, waiting for transfers between devices, along(): lax.ppermute(block, 'dp', [(2 * a + s, 2 * b + s) for a, b in hops for s...  26.9 us
    ppermute x5, starting transfers between devices, along(): lax.ppermute(block, 'dp', [(2 * a + s, 2 * b + s) for a, b in hops for s...  9.84 us
    pallas_call x1, Pallas kernels, project_early(): pl.pallas_call(functools.partial(early_kernel, blocks), out_shape=[jax.Sh...  7.82 us
    pallas_call x1, Pallas kernels, project_late_attend(): pl.pallas_call(functools.partial(late_kernel, blocks), out_shape=[queries...  7.2 us
    ppermute x4, starting transfers between devices, across(): lax.ppermute(block, 'dp', [(2 * a + s, 2 * a + 1 - s) for a in places for...  6.27 us
    pallas_call x1, Pallas kernels, attend_own(): pl.pallas_call(own_kernel, out_shape=jax.ShapeDtypeStruct((rows, width),...  5.18 us
    ppermute x4, waiting for transfers between devices, across(): lax.ppermute(block, 'dp', [(2 * a + s, 2 * a + 1 - s) for a in places for...  3.07 us
    ppermute x1, starting transfers between devices, local(): lax.ppermute(partner_out, 'tm', [(i, i ^ 1) for i in range(members)])  2.66 us
  transfers between devices with their start and end apart: 13, of which 6 were waited for; matrix products, arithmetic and copies ran while one was open for 0% of the time, Pallas kernels for 27%

profile of v2, /device:TPU:0, one launch (start us, length us, event | category | flops | bytes accessed | tf_op | source)
XLA Modules:
  0.0 76.0 jit_solution(17400426780923050591)
XLA Ops:
  0.0 1.3 %slice_select_fusion.2 = (bf16[192,384]{1,0:T(8,128)(2,1)S(1)}, bf16[192,384]{1,0:T(8,128)(2,1)S(1)}, bf16[192,384]{1,0:T(8,128)(2,1)S(1)}) fusion(bf16[192,2304]{1,0:T(8,128)(2,1)} %param.6, pred[]{:T(512)S(6)} %eq.4), kind=kLoop, calls=%fused_computation.6 | loop fusion | flops 221184 | bytes 1327105 | tf_op jit(solution)/shard_map/jit(_where)/select_n | solution.py:402
  1.4 0.7 collective-permute-start.2
  2.1 5.9 %collective-permute-start.1 = (bf16[192,1152]{1,0:T(8,128)(2,1)S(1)}, bf16[192,1152]{1,0:T(8,128)(2,1)S(1)}, u32[]{:S(2)}, u32[]{:S(2)}) collective-permute-start(bf16[192,1152]{1,0:T(8,128)(2,1)S(1)} %pad_maximum_fusion.refs_0_), channel_id=1, source_target_pairs={{8,0},{12,4},{16,24},{20,28},{0,8},{4,12},{24,16},{28,20},{9,1},{1... | collective-permute-start | bytes 1327112 | tf_op jit(solution)/shard_map/near/ppermute | solution.py:343
  7.9 1.5 %collective-permute-start = (bf16[192,1152]{1,0:T(8,128)(2,1)S(1)}, bf16[192,1152]{1,0:T(8,128)(2,1)S(1)}, u32[]{:S(2)}, u32[]{:S(2)}) collective-permute-start(bf16[192,1152]{1,0:T(8,128)(2,1)S(1)} %pad_maximum_fusion.refs_0_), channel_id=1, source_target_pairs={{0,4},{4,0},{8,12},{12,8},{16,20},{20,16},{24,28},{28,24},{1,5},{5... | collective-permute-start | bytes 1327112 | tf_op jit(solution)/shard_map/half_across/ppermute | solution.py:349
  9.5 0.0 collective-permute-start.9
  9.5 0.0 collective-permute-done.2.between_ref
  9.5 8.4 %collective-permute-done.1.refs_2_ = bf16[192,1152]{1,0:T(8,128)(2,1)S(1)} collective-permute-done((bf16[192,1152]{1,0:T(8,128)(2,1)S(1)}, bf16[192,1152]{1,0:T(8,128)(2,1)S(1)}, u32[]{:S(2)}, u32[]{:S(2)}) %collective-permute-start.1) | collective-permute-done | bytes 442400 | tf_op jit(solution)/shard_map/near/ppermute | solution.py:343
  17.8 1.5 %collective-permute-done.refs_1_ = bf16[192,1152]{1,0:T(8,128)(2,1)S(1)} collective-permute-done((bf16[192,1152]{1,0:T(8,128)(2,1)S(1)}, bf16[192,1152]{1,0:T(8,128)(2,1)S(1)}, u32[]{:S(2)}, u32[]{:S(2)}) %collective-permute-start) | collective-permute-done | bytes 442400 | tf_op jit(solution)/shard_map/half_across/ppermute | solution.py:349
  19.3 1.3 %collective-permute-start.4 = (bf16[192,1152]{1,0:T(8,128)(2,1)S(1)}, bf16[192,1152]{1,0:T(8,128)(2,1)S(1)}, u32[]{:S(2)}, u32[]{:S(2)}) collective-permute-start(bf16[192,1152]{1,0:T(8,128)(2,1)S(1)} %collective-permute-done.2.between_ref), channel_id=1, source_target_pairs={{8,0},{12,4},{16,24},{20,28},{9,1},{13,5},{17,25},{21,29},{10,2},{... | collective-permute-start | bytes 1327112 | tf_op jit(solution)/shard_map/end_mid/ppermute | solution.py:343
  20.6 0.7 collective-permute-start.6
  21.3 1.6 %collective-permute-start.3 = (bf16[192,1152]{1,0:T(8,128)(2,1)S(1)}, bf16[192,1152]{1,0:T(8,128)(2,1)S(1)}, u32[]{:S(2)}, u32[]{:S(2)}) collective-permute-start(bf16[192,1152]{1,0:T(8,128)(2,1)S(1)} %collective-permute-done.1.refs_2_), channel_id=1, source_target_pairs={{0,4},{4,0},{8,12},{12,8},{16,20},{20,16},{24,28},{28,24},{1,5},{5... | collective-permute-start | bytes 1327112 | tf_op jit(solution)/shard_map/near_across/ppermute | solution.py:349
  22.9 0.0 copy-start
  22.9 1.7 %copy-done = bf16[1,768,1536]{2,1,0:T(8,128)(2,1)S(1)} copy-done((bf16[1,768,1536]{2,1,0:T(8,128)(2,1)S(1)}, bf16[1,768,1536]{2,1,0:T(8,128)(2,1)}, u32[]{:S(2)}) %copy-start) | copy-done | bytes 2359320
  24.5 0.1 take_tail.1
  24.6 0.0 copy-start.1
  24.7 6.9 %collective-permute-done.4.end_ref = bf16[192,1152]{1,0:T(8,128)(2,1)S(1)} collective-permute-done((bf16[192,1152]{1,0:T(8,128)(2,1)S(1)}, bf16[192,1152]{1,0:T(8,128)(2,1)S(1)}, u32[]{:S(2)}, u32[]{:S(2)}) %collective-permute-start.4) | collective-permute-done | bytes 442400 | tf_op jit(solution)/shard_map/end_mid/ppermute | solution.py:343
  31.6 0.0 collective-permute-done.6.between_ref
  31.6 0.2 collective-permute-done.3.refs_3_
  31.8 0.8 collective-permute-start.10
  32.5 1.3 %collective-permute-start.7 = (bf16[192,1152]{1,0:T(8,128)(2,1)S(1)}, bf16[192,1152]{1,0:T(8,128)(2,1)S(1)}, u32[]{:S(2)}, u32[]{:S(2)}) collective-permute-start(bf16[192,1152]{1,0:T(8,128)(2,1)S(1)} %collective-permute-done.6.between_ref), channel_id=1, source_target_pairs={{8,0},{12,4},{16,24},{20,28},{9,1},{13,5},{17,25},{21,29},{10,2},{... | collective-permute-start | bytes 1327112 | tf_op jit(solution)/shard_map/end_far/ppermute | solution.py:343
  33.8 0.3 choose.2.refs_4_
  34.1 1.6 %collective-permute-start.5 = (bf16[192,1152]{1,0:T(8,128)(2,1)S(1)}, bf16[192,1152]{1,0:T(8,128)(2,1)S(1)}, u32[]{:S(2)}, u32[]{:S(2)}) collective-permute-start(bf16[192,1152]{1,0:T(8,128)(2,1)S(1)} %choose.2.refs_4_), channel_id=1, source_target_pairs={{0,4},{4,0},{8,12},{12,8},{16,20},{20,16},{24,28},{28,24},{1,5},{5... | collective-permute-start | bytes 1327112 | tf_op jit(solution)/shard_map/second_across/ppermute | solution.py:349
  35.7 11.6 %collective-permute-done.7.end_ref = bf16[192,1152]{1,0:T(8,128)(2,1)S(1)} collective-permute-done((bf16[192,1152]{1,0:T(8,128)(2,1)S(1)}, bf16[192,1152]{1,0:T(8,128)(2,1)S(1)}, u32[]{:S(2)}, u32[]{:S(2)}) %collective-permute-start.7) | collective-permute-done | bytes 442400 | tf_op jit(solution)/shard_map/end_far/ppermute | solution.py:343
  47.2 0.3 choose.3.refs_6_
  47.5 0.0 copy-start.2
  47.5 0.0 copy-start.3
  47.5 0.0 copy-start.4
  47.5 0.0 collective-permute-done.5.refs_5_
  47.6 1.6 %collective-permute-start.8 = (bf16[192,1152]{1,0:T(8,128)(2,1)S(1)}, bf16[192,1152]{1,0:T(8,128)(2,1)S(1)}, u32[]{:S(2)}, u32[]{:S(2)}) collective-permute-start(bf16[192,1152]{1,0:T(8,128)(2,1)S(1)} %choose.3.refs_6_), channel_id=1, source_target_pairs={{0,4},{4,0},{8,12},{12,8},{16,20},{20,16},{24,28},{28,24},{1,5},{5... | collective-permute-start | bytes 1327112 | tf_op jit(solution)/shard_map/third_across/ppermute | solution.py:349
  49.1 0.0 collective-permute-done.9.refs_7_.refs_9_
  49.1 0.0 copy-done.1
  49.2 7.8 %project_early.1 = (f32[768,1152]{1,0:T(8,128)S(1)}, f32[768,1152]{1,0:T(8,128)S(1)}) custom-call(bf16[192,1152]{1,0:T(8,128)(2,1)S(1)} %pad_maximum_fusion.refs_0_, bf16[192,1152]{1,0:T(8,128)(2,1)S(1)} %collective-permute-done.refs_1_, bf16[192,1152]{1,0:T(8,128)(2,1)S(1)} %collective-permute-done.1.refs_2_, ...), custom_call_target="tpu_custom_call" | custom-call | tf_op jit(solution)/shard_map/project_early/pallas_call | solution.py:238
  57.0 1.4 %collective-permute-done.8.refs_7_ = bf16[192,1152]{1,0:T(8,128)(2,1)S(1)} collective-permute-done((bf16[192,1152]{1,0:T(8,128)(2,1)S(1)}, bf16[192,1152]{1,0:T(8,128)(2,1)S(1)}, u32[]{:S(2)}, u32[]{:S(2)}) %collective-permute-start.8) | collective-permute-done | bytes 442400 | tf_op jit(solution)/shard_map/third_across/ppermute | solution.py:349
  58.4 0.0 collective-permute-done.10.refs_10_
  58.4 1.3 %collective-permute-start.11 = (bf16[512,1536]{1,0:T(8,128)(2,1)S(1)}, bf16[512,1536]{1,0:T(8,128)(2,1)S(1)}, u32[]{:S(2)}, u32[]{:S(2)}) collective-permute-start(bf16[512,1536]{1,0:T(8,128)(2,1)S(1)} %collective-permute-done.10.refs_10_), channel_id=1, source_target_pairs={{1,0},{3,2},{5,4},{7,6},{9,8},{11,10},{13,12},{15,14},{17,16},{19,... | collective-permute-start | bytes 4718600 | tf_op jit(solution)/shard_map/halo_first/ppermute | solution.py:425
  59.7 0.0 copy-done.2
  59.7 0.0 copy-done.3
  59.7 0.0 copy-done.4
  59.7 7.2 %project_late_attend.1 = (bf16[768,384]{1,0:T(8,128)(2,1)S(1)}, bf16[768,384]{1,0:T(8,128)(2,1)S(1)}, bf16[2048,384]{1,0:T(8,128)(2,1)S(1)}, bf16[2048,384]{1,0:T(8,128)(2,1)S(1)}, bf16[1536,768]{1,0:T(8,128)(2,1)S(1)}) custom-call(s32[1,3]{1,0:T(1,128)S(1)} %copy-done.2, s32[1,12]{1,0:T(1,128)S(1)} %copy-done.3, s32[1,12]{1,0:T(1,128)S(1)} %copy-done.4, ...), custom_call_target="tpu_custom_call" | custom-call | tf_op jit(solution)/shard_map/project_late_attend/pallas_call | solution.py:280
  67.0 2.7 %collective-permute-start.12 = (bf16[768,384]{1,0:T(8,128)(2,1)S(1)}, bf16[768,384]{1,0:T(8,128)(2,1)S(1)}, u32[]{:S(2)}, u32[]{:S(2)}) collective-permute-start(bf16[768,384]{1,0:T(8,128)(2,1)S(1)} %get-tuple-element.32), channel_id=1, source_target_pairs={{0,1},{1,0},{2,3},{3,2},{4,5},{5,4},{6,7},{7,6},{8,9},{9,8},{10,11... | collective-permute-start | bytes 1769480 | tf_op jit(solution)/shard_map/swap/ppermute | solution.py:432
  69.6 0.0 collective-permute-done.11.halo_ref
  69.6 5.2 %attend_own.1 = bf16[768,384]{1,0:T(8,128)(2,1)S(1)} custom-call(s32[1,3]{1,0:T(1,128)S(1)} %copy-done.2, s32[1,12]{1,0:T(1,128)S(1)} %copy-done.3, s32[1,12]{1,0:T(1,128)S(1)} %copy-done.4, bf16[768,384]{1,0:T(8,128)(2,1)S(1)} %get-tuple-element.27.q_ref, bf16[2048,384]{1,0:T(8,128)(2,1)S(1)} %get-tuple-element.28.k_ref, ...), custom_call_target="tpu_custom_call" | custom-call | tf_op jit(solution)/shard_map/attend_own/pallas_call | solution.py:305
  74.8 0.0 collective-permute-done.12
  74.8 0.1 broadcast_select_fusion.1
  74.9 1.1 %maximum_bitcast_fusion = bf16[1,768,768]{2,1,0:T(8,128)(2,1)} fusion(bf16[768,384]{1,0:T(8,128)(2,1)S(1)} %get-tuple-element.34, bf16[768,384]{1,0:T(8,128)(2,1)S(1)} %get-tuple-element.33), kind=kLoop, calls=%fused_computation | loop fusion | flops 2359296 | bytes 2359296 | tf_op jit(solution)/shard_map/broadcast_in_dim | solution.py:436
  (1 shorter events, 0.0 us)
Async XLA Ops:
  1.4 8.1 %collective-permute-start.2 = (bf16[192,1152]{1,0:T(8,128)(2,1)S(1)}, bf16[192,1152]{1,0:T(8,128)(2,1)S(1)}, u32[]{:S(2)}, u32[]{:S(2)}) collective-permute-start(bf16[192,1152]{1,0:T(8,128)(2,1)S(1)} %pad_maximum_fusion.refs_0_), channel_id=1, source_target_pairs={{8,16},{12,20},{16,8},{20,12},{9,17},{13,21},{17,9},{21,13},{10,18... | collective-permute-start | bytes 1327112 | tf_op jit(solution)/shard_map/mid/ppermute | solution.py:343
  2.1 15.8 %collective-permute-start.1 = (bf16[192,1152]{1,0:T(8,128)(2,1)S(1)}, bf16[192,1152]{1,0:T(8,128)(2,1)S(1)}, u32[]{:S(2)}, u32[]{:S(2)}) collective-permute-start(bf16[192,1152]{1,0:T(8,128)(2,1)S(1)} %pad_maximum_fusion.refs_0_), channel_id=1, source_target_pairs={{8,0},{12,4},{16,24},{20,28},{0,8},{4,12},{24,16},{28,20},{9,1},{1... | collective-permute-start | bytes 1327112 | tf_op jit(solution)/shard_map/near/ppermute | solution.py:343
  7.9 11.3 %collective-permute-start = (bf16[192,1152]{1,0:T(8,128)(2,1)S(1)}, bf16[192,1152]{1,0:T(8,128)(2,1)S(1)}, u32[]{:S(2)}, u32[]{:S(2)}) collective-permute-start(bf16[192,1152]{1,0:T(8,128)(2,1)S(1)} %pad_maximum_fusion.refs_0_), channel_id=1, source_target_pairs={{0,4},{4,0},{8,12},{12,8},{16,20},{20,16},{24,28},{28,24},{1,5},{5... | collective-permute-start | bytes 1327112 | tf_op jit(solution)/shard_map/half_across/ppermute | solution.py:349
  9.5 39.7 %collective-permute-start.9 = (bf16[768,1536]{1,0:T(8,128)(2,1)}, bf16[768,1536]{1,0:T(8,128)(2,1)S(1)}, u32[]{:S(2)}, u32[]{:S(2)}) collective-permute-start(bf16[768,1536]{1,0:T(8,128)(2,1)} %bitcast.3), channel_id=1, source_target_pairs={{0,1},{1,0},{2,3},{3,2},{4,5},{5,4},{6,7},{7,6},{8,9},{9,8},{10,11... | collective-permute-start | bytes 7077896 | tf_op jit(solution)/shard_map/partner/ppermute | solution.py:407
  19.3 12.3 %collective-permute-start.4 = (bf16[192,1152]{1,0:T(8,128)(2,1)S(1)}, bf16[192,1152]{1,0:T(8,128)(2,1)S(1)}, u32[]{:S(2)}, u32[]{:S(2)}) collective-permute-start(bf16[192,1152]{1,0:T(8,128)(2,1)S(1)} %collective-permute-done.2.between_ref), channel_id=1, source_target_pairs={{8,0},{12,4},{16,24},{20,28},{9,1},{13,5},{17,25},{21,29},{10,2},{... | collective-permute-start | bytes 1327112 | tf_op jit(solution)/shard_map/end_mid/ppermute | solution.py:343
  20.6 11.0 %collective-permute-start.6 = (bf16[192,1152]{1,0:T(8,128)(2,1)S(1)}, bf16[192,1152]{1,0:T(8,128)(2,1)S(1)}, u32[]{:S(2)}, u32[]{:S(2)}) collective-permute-start(bf16[192,1152]{1,0:T(8,128)(2,1)S(1)} %collective-permute-done.1.refs_2_), channel_id=1, source_target_pairs={{8,16},{12,20},{16,8},{20,12},{9,17},{13,21},{17,9},{21,13},{10,18... | collective-permute-start | bytes 1327112 | tf_op jit(solution)/shard_map/mid_far/ppermute | solution.py:343
  21.3 10.5 %collective-permute-start.3 = (bf16[192,1152]{1,0:T(8,128)(2,1)S(1)}, bf16[192,1152]{1,0:T(8,128)(2,1)S(1)}, u32[]{:S(2)}, u32[]{:S(2)}) collective-permute-start(bf16[192,1152]{1,0:T(8,128)(2,1)S(1)} %collective-permute-done.1.refs_2_), channel_id=1, source_target_pairs={{0,4},{4,0},{8,12},{12,8},{16,20},{20,16},{24,28},{28,24},{1,5},{5... | collective-permute-start | bytes 1327112 | tf_op jit(solution)/shard_map/near_across/ppermute | solution.py:349
  22.9 1.7 %copy-start = (bf16[1,768,1536]{2,1,0:T(8,128)(2,1)S(1)}, bf16[1,768,1536]{2,1,0:T(8,128)(2,1)}, u32[]{:S(2)}) copy-start(bf16[1,768,1536]{2,1,0:T(8,128)(2,1)} %param.5) | copy-start | bytes 7077892
  24.6 24.5 %copy-start.1 = (bf16[1,768,1536]{2,1,0:T(8,128)(2,1)S(1)}, bf16[1,768,1536]{2,1,0:T(8,128)(2,1)}, u32[]{:S(2)}) copy-start(bf16[1,768,1536]{2,1,0:T(8,128)(2,1)} %param.5) | copy-start | bytes 7077892
  31.8 26.7 %collective-permute-start.10 = (bf16[512,1536]{1,0:T(8,128)(2,1)S(1)}, bf16[512,1536]{1,0:T(8,128)(2,1)S(1)}, u32[]{:S(2)}, u32[]{:S(2)}) collective-permute-start(bf16[512,1536]{1,0:T(8,128)(2,1)S(1)} %take_tail.1), channel_id=1, source_target_pairs={{1,3},{5,7},{9,11},{13,15},{17,19},{21,23},{25,27},{29,31}} | collective-permute-start | bytes 4718600 | tf_op jit(solution)/shard_map/halo/ppermute | solution.py:418
  32.5 14.7 %collective-permute-start.7 = (bf16[192,1152]{1,0:T(8,128)(2,1)S(1)}, bf16[192,1152]{1,0:T(8,128)(2,1)S(1)}, u32[]{:S(2)}, u32[]{:S(2)}) collective-permute-start(bf16[192,1152]{1,0:T(8,128)(2,1)S(1)} %collective-permute-done.6.between_ref), channel_id=1, source_target_pairs={{8,0},{12,4},{16,24},{20,28},{9,1},{13,5},{17,25},{21,29},{10,2},{... | collective-permute-start | bytes 1327112 | tf_op jit(solution)/shard_map/end_far/ppermute | solution.py:343
  34.1 13.4 %collective-permute-start.5 = (bf16[192,1152]{1,0:T(8,128)(2,1)S(1)}, bf16[192,1152]{1,0:T(8,128)(2,1)S(1)}, u32[]{:S(2)}, u32[]{:S(2)}) collective-permute-start(bf16[192,1152]{1,0:T(8,128)(2,1)S(1)} %choose.2.refs_4_), channel_id=1, source_target_pairs={{0,4},{4,0},{8,12},{12,8},{16,20},{20,16},{24,28},{28,24},{1,5},{5... | collective-permute-start | bytes 1327112 | tf_op jit(solution)/shard_map/second_across/ppermute | solution.py:349
  47.5 12.2 %copy-start.2 = (s32[1,3]{1,0:T(1,128)S(1)}, s32[1,3]{1,0:T(1,128)}, u32[]{:S(2)}) copy-start(s32[1,3]{1,0:T(1,128)} %start_ref.3) | copy-start | bytes 40
  47.5 12.2 %copy-start.3 = (s32[1,12]{1,0:T(1,128)S(1)}, s32[1,12]{1,0:T(1,128)}, u32[]{:S(2)}) copy-start(s32[1,12]{1,0:T(1,128)} %owner_ref.3) | copy-start | bytes 148
  47.5 12.2 %copy-start.4 = (s32[1,12]{1,0:T(1,128)S(1)}, s32[1,12]{1,0:T(1,128)}, u32[]{:S(2)}) copy-start(s32[1,12]{1,0:T(1,128)} %left_ref.3) | copy-start | bytes 148
  47.6 10.9 %collective-permute-start.8 = (bf16[192,1152]{1,0:T(8,128)(2,1)S(1)}, bf16[192,1152]{1,0:T(8,128)(2,1)S(1)}, u32[]{:S(2)}, u32[]{:S(2)}) collective-permute-start(bf16[192,1152]{1,0:T(8,128)(2,1)S(1)} %choose.3.refs_6_), channel_id=1, source_target_pairs={{0,4},{4,0},{8,12},{12,8},{16,20},{20,16},{24,28},{28,24},{1,5},{5... | collective-permute-start | bytes 1327112 | tf_op jit(solution)/shard_map/third_across/ppermute | solution.py:349
  58.4 11.2 %collective-permute-start.11 = (bf16[512,1536]{1,0:T(8,128)(2,1)S(1)}, bf16[512,1536]{1,0:T(8,128)(2,1)S(1)}, u32[]{:S(2)}, u32[]{:S(2)}) collective-permute-start(bf16[512,1536]{1,0:T(8,128)(2,1)S(1)} %collective-permute-done.10.refs_10_), channel_id=1, source_target_pairs={{1,0},{3,2},{5,4},{7,6},{9,8},{11,10},{13,12},{15,14},{17,16},{19,... | collective-permute-start | bytes 4718600 | tf_op jit(solution)/shard_map/halo_first/ppermute | solution.py:425
  67.0 7.9 %collective-permute-start.12 = (bf16[768,384]{1,0:T(8,128)(2,1)S(1)}, bf16[768,384]{1,0:T(8,128)(2,1)S(1)}, u32[]{:S(2)}, u32[]{:S(2)}) collective-permute-start(bf16[768,384]{1,0:T(8,128)(2,1)S(1)} %get-tuple-element.32), channel_id=1, source_target_pairs={{0,1},{1,0},{2,3},{3,2},{4,5},{5,4},{6,7},{7,6},{8,9},{9,8},{10,11... | collective-permute-start | bytes 1769480 | tf_op jit(solution)/shard_map/swap/ppermute | solution.py:432

commit v3 on v1

--- a/solution.py
+++ b/solution.py
@@ -240,6 +240,55 @@
 SMEM_SPEC = pl.BlockSpec(memory_space=pltpu.SMEM)
 VMEM_SPEC = pl.BlockSpec(memory_space=pltpu.VMEM)
 ANY_SPEC = pl.BlockSpec(memory_space=pl.ANY)
+
+
+def half_kernel(w_ref, out_ref, sems):
+    width = out_ref.shape[1] // 3
+    core = lax.axis_index("tm") % 2
+    pairs = []
+    for third in range(3):
+        at = pl.multiple_of((2 * third + core) * width, LANES)
+        pairs.append((w_ref.at[:, pl.ds(at, width)], out_ref.at[:, third * width : (third + 1) * width]))
+    for copy in start_all(sems, pairs):
+        copy.wait()
+
+
+def take_half(w):
+    return pl.pallas_call(
+        half_kernel,
+        out_shape=jax.ShapeDtypeStruct((w.shape[0], w.shape[1] // 2), w.dtype),
+        in_specs=[pl.BlockSpec(memory_space=pltpu.HBM)],
+        out_specs=VMEM_SPEC,
+        scratch_shapes=[pltpu.SemaphoreType.DMA((3,))],
+        compiler_params=pltpu.CompilerParams(vmem_limit_bytes=4 * MIB),
+        name="take_half",
+    )(w)
+
+
+def join_kernel(own_ref, other_ref, out_ref, sems):
+    rows, width = own_ref.shape
+    core = lax.axis_index("tm") % 2
+    own_at = pl.multiple_of(core * width, LANES)
+    other_at = pl.multiple_of((1 - core) * width, LANES)
+    pairs = [
+        (own_ref, out_ref.at[:, pl.ds(own_at, width)]),
+        (other_ref.at[:rows, :], out_ref.at[:, pl.ds(other_at, width)]),
+    ]
+    for copy in start_all(sems, pairs):
+        copy.wait()
+
+
+def join(own, other):
+    rows, width = own.shape
+    return pl.pallas_call(
+        join_kernel,
+        out_shape=jax.ShapeDtypeStruct((rows, 2 * width), own.dtype),
+        in_specs=[ANY_SPEC] * 2,
+        out_specs=ANY_SPEC,
+        scratch_shapes=[pltpu.SemaphoreType.DMA((2,))],
+        compiler_params=pltpu.CompilerParams(vmem_limit_bytes=4 * MIB),
+        name="join",
+    )(own, other)
 
 
 def project_early(blocks, inputs, partner):
@@ -324,7 +373,29 @@
     )(*tables, queries, keys, values, weights, halo, done)
 
 
-def gather_neighbours(half, tail):
+def at_end():
+    place = lax.axis_index("dp") // 2
+    return jnp.where((place == 0) | (place == 3), 1, 0)
+
+
+def choose_kernel(between_ref, end_ref, out_ref, sems):
+    for copy in start_all(sems, [((between_ref, end_ref), at_end(), out_ref)]):
+        copy.wait()
+
+
+def choose(between, end):
+    return pl.pallas_call(
+        choose_kernel,
+        out_shape=jax.ShapeDtypeStruct(end.shape, end.dtype),
+        in_specs=[ANY_SPEC] * 2,
+        out_specs=VMEM_SPEC,
+        scratch_shapes=[pltpu.SemaphoreType.DMA((1,))],
+        compiler_params=pltpu.CompilerParams(vmem_limit_bytes=2 * MIB),
+        name="choose",
+    )(between, end)
+
+
+def gather_neighbours(half):
     size = half.shape[0]
 
     def along(name, block, hops):
@@ -339,25 +410,25 @@
                 block, "dp", [(2 * a + s, 2 * a + 1 - s) for a in places for s in range(2)]
             )
 
-    line, ends, middles = range(4), (0, 3), (1, 2)
+    line = range(4)
     outward = [(1, 0), (2, 3)]
     between = [(1, 2), (2, 1)]
     near = along("near", half, outward + [(0, 1), (3, 2)])
-    mid = along("mid", after(half, tail), between)
+    mid = along("mid", half, between)
     half_across = across("half_across", half, line)
     mid_far = along("mid_far", near, between)
     near_across = across("near_across", after(near, half_across, mid), line)
     end_mid = along("end_mid", mid, outward)
-    mid_across = across("mid_across", after(mid, near_across, mid_far), middles)
-    end_mid_across = across("end_mid_across", after(end_mid, near_across), ends)
     end_far = along("end_far", after(mid_far, end_mid), outward)
-    mid_far_across = across("mid_far_across", after(mid_far, mid_across, end_far), middles)
-    end_far_across = across("end_far_across", after(end_far, near_across), ends)
+    second = choose(mid, end_mid)
+    second_across = across("second_across", after(second, near_across), line)
+    third = choose(mid_far, end_far)
+    third_across = across("third_across", after(third, second_across), line)
 
     def find():
         index = lax.axis_index("dp")
         place, side = index // 2, index % 2
-        is_end = jnp.where((place == 0) | (place == 3), 1, 0)
+        is_end = at_end()
         second = jnp.where(is_end == 1, place ^ 2, 3 - place)
         third = jnp.where(is_end == 1, 3 - place, place ^ 2)
         spots = (place, place ^ 1, second, third)
@@ -369,16 +440,12 @@
         (half_across,),
         (near,),
         (near_across,),
-        (mid, end_mid),
-        (mid_across, end_mid_across),
-        (mid_far, end_far),
-        (mid_far_across, end_far_across),
+        (second,),
+        (second_across,),
+        (third,),
+        (third_across,),
     ]
-    marks = (
-        (near_across, mid_far, end_mid),
-        (mid_across, end_mid_across, end_far),
-        (mid_far_across, end_far_across),
-    )
+    marks = (near_across, mid_far, end_mid), (second_across, end_far), (third_across,)
     return Blocks(blocks, 2, find), marks
 
 
@@ -386,20 +453,14 @@
     inputs = frames[0]
     depth = inputs.shape[1]
     members = lax.axis_size("tm")
-    core = lax.axis_index("tm") % 2
-
-    inner = w_qkv.shape[1] // 3
-    width = inner // 2
-    thirds = [w_qkv[:, i * inner : (i + 1) * inner] for i in range(3)]
-    half = jnp.concatenate(
-        [jnp.where(core == 0, third[:, :width], third[:, width:]) for third in thirds], axis=1
-    )
+
+    half = take_half(w_qkv)
 
     tail = take_tail(after(inputs, half))
     with jax.named_scope("partner"):
         partner = lax.ppermute(inputs, "tm", [(i, i ^ 1) for i in range(members)])
     if lax.axis_size("dp") == 8:
-        blocks, marks = gather_neighbours(half, tail)
+        blocks, marks = gather_neighbours(half)
     else:
         weights = lax.all_gather(half, "dp", axis=0, tiled=True)
         late_first = depth - depth // GROUPS
@@ -424,10 +485,7 @@
     with jax.named_scope("swap"):
         other = lax.ppermute(attended, "tm", [(i, i ^ 1) for i in range(members)])
     own_out = attend_own(tables, queries, keys, values, weights, halo_first, attended)
-    other = other[: inputs.shape[0]]
-    left = jnp.where(core == 0, own_out, other)
-    right = jnp.where(core == 0, other, own_out)
-    return jnp.concatenate([left, right], axis=1)[None]
+    return join(own_out, other)[None]
 
 
 def solution(mesh):

time: 81.1 us -> 76.5 us (0.943)
  starting transfers between devices: 22.1 us -> 16.1 us
  other arithmetic: 2.57 us -> 0 us
  waiting for transfers between devices: 33.4 us -> 34.6 us
  Pallas kernels: 20.8 us -> 22 us
  local copies, waits for them, and re-layouts: 1.69 us -> 2.85 us
    ppermute x6 -> x4, waiting for transfers between devices: 10.7 us -> 16.5 us  [across(): lax.ppermute(block, 'dp', [(2 * a + s, 2 * a + 1 - s) for a in places for...]
    ppermute x6 -> x4, starting transfers between devices: 11.3 us -> 6.56 us  [across(): lax.ppermute(block, 'dp', [(2 * a + s, 2 * a + 1 - s) for a in places for...]
    ppermute x5, waiting for transfers between devices: 22.7 us -> 18.1 us  [along(): lax.ppermute(block, 'dp', [(2 * a + s, 2 * b + s) for a, b in hops for s...]
    pallas_call x0 -> x4, Pallas kernels: none -> 1.66 us  [the longest x1 1.04 us: join(): pl.pallas_call(join_kernel, out_shape=jax.ShapeDtypeStruct((rows, 2 * wid...]
    ppermute x5, starting transfers between devices: 7.16 us -> 5.51 us  [along(): lax.ppermute(block, 'dp', [(2 * a + s, 2 * b + s) for a, b in hops for s...]
    select_n x2 -> x0, other arithmetic: 1.42 us -> none  [the longest x1 1.31 us: local(): jnp.where(core == 0, third[:, :width], third[:, width:])]
    unnamed x10 -> x12, local copies, waits for them, and re-layouts: 1.69 us -> 2.85 us
    broadcast_in_dim x1 -> x0, other arithmetic: 1.11 us -> none  [local(): return jnp.concatenate([left, right], axis=1)[None]]
  transfers between devices with their start and end apart: 15 -> 13, of which waited for: 6 -> 6; matrix products, arithmetic and copies ran while one was open for 0% -> 0% of each run, Pallas kernels for 26% -> 27%
where the time goes in v3:
time: 76.5 us; the launch traced here: 75.9 us
  waiting for transfers between devices  34.6 us (45%)
  Pallas kernels  22 us (29%)
  starting transfers between devices  16.1 us (21%)
  local copies, waits for them, and re-layouts  2.85 us (4%)
    ppermute x5, waiting for transfers between devices, along(): lax.ppermute(block, 'dp', [(2 * a + s, 2 * b + s) for a, b in hops for s...  18.1 us
    ppermute x4, waiting for transfers between devices, across(): lax.ppermute(block, 'dp', [(2 * a + s, 2 * a + 1 - s) for a in places for...  16.5 us
    pallas_call x1, Pallas kernels, project_late_attend(): pl.pallas_call(functools.partial(late_kernel, blocks), out_shape=[jax.Sha...  7.98 us
    pallas_call x1, Pallas kernels, project_early(): pl.pallas_call(functools.partial(early_kernel, blocks), out_shape=[jax.Sh...  7.82 us
    ppermute x4, starting transfers between devices, across(): lax.ppermute(block, 'dp', [(2 * a + s, 2 * a + 1 - s) for a in places for...  6.56 us
    ppermute x5, starting transfers between devices, along(): lax.ppermute(block, 'dp', [(2 * a + s, 2 * b + s) for a, b in hops for s...  5.51 us
    pallas_call x1, Pallas kernels, attend_own(): pl.pallas_call(own_kernel, out_shape=jax.ShapeDtypeStruct((rows, width),...  4.42 us
    unnamed x12, local copies, waits for them, and re-layouts  2.85 us
  transfers between devices with their start and end apart: 13, of which 6 were waited for; matrix products, arithmetic and copies ran while one was open for 0% of the time, Pallas kernels for 27%

profile of v3, /device:TPU:0, one launch (start us, length us, event | category | flops | bytes accessed | tf_op | source)
XLA Modules:
  0.0 75.9 jit_solution(3793669670160406103)
XLA Ops:
  0.0 0.0 copy-start.2
  0.0 1.2 %copy-done.2 = bf16[192,2304]{1,0:T(8,128)(2,1)S(1)} copy-done((bf16[192,2304]{1,0:T(8,128)(2,1)S(1)}, bf16[192,2304]{1,0:T(8,128)(2,1)}, u32[]{:S(2)}) %copy-start.2) | copy-done | bytes 884760
  1.2 0.1 take_half.1.refs_0_
  1.3 3.0 %collective-permute-start = (bf16[192,1152]{1,0:T(8,128)(2,1)S(1)}, bf16[192,1152]{1,0:T(8,128)(2,1)S(1)}, u32[]{:S(2)}, u32[]{:S(2)}) collective-permute-start(bf16[192,1152]{1,0:T(8,128)(2,1)S(1)} %take_half.1.refs_0_), channel_id=1, source_target_pairs={{0,4},{4,0},{8,12},{12,8},{16,20},{20,16},{24,28},{28,24},{1,5},{5... | collective-permute-start | bytes 1327112 | tf_op jit(solution)/shard_map/half_across/ppermute | solution.py:409
  4.3 1.6 %collective-permute-start.1 = (bf16[192,1152]{1,0:T(8,128)(2,1)S(1)}, bf16[192,1152]{1,0:T(8,128)(2,1)S(1)}, u32[]{:S(2)}, u32[]{:S(2)}) collective-permute-start(bf16[192,1152]{1,0:T(8,128)(2,1)S(1)} %take_half.1.refs_0_), channel_id=1, source_target_pairs={{8,0},{12,4},{16,24},{20,28},{0,8},{4,12},{24,16},{28,20},{9,1},{1... | collective-permute-start | bytes 1327112 | tf_op jit(solution)/shard_map/near/ppermute | solution.py:403
  5.9 0.7 collective-permute-start.2
  6.5 0.1 collective-permute-start.9
  6.6 7.8 %collective-permute-done.refs_1_ = bf16[192,1152]{1,0:T(8,128)(2,1)S(1)} collective-permute-done((bf16[192,1152]{1,0:T(8,128)(2,1)S(1)}, bf16[192,1152]{1,0:T(8,128)(2,1)S(1)}, u32[]{:S(2)}, u32[]{:S(2)}) %collective-permute-start) | collective-permute-done | bytes 442400 | tf_op jit(solution)/shard_map/half_across/ppermute | solution.py:409
  14.5 1.5 %collective-permute-done.1.refs_2_ = bf16[192,1152]{1,0:T(8,128)(2,1)S(1)} collective-permute-done((bf16[192,1152]{1,0:T(8,128)(2,1)S(1)}, bf16[192,1152]{1,0:T(8,128)(2,1)S(1)}, u32[]{:S(2)}, u32[]{:S(2)}) %collective-permute-start.1) | collective-permute-done | bytes 442400 | tf_op jit(solution)/shard_map/near/ppermute | solution.py:403
  15.9 0.0 collective-permute-done.2.between_ref
  15.9 0.4 collective-permute-start.3
  16.3 1.3 %collective-permute-start.4 = (bf16[192,1152]{1,0:T(8,128)(2,1)S(1)}, bf16[192,1152]{1,0:T(8,128)(2,1)S(1)}, u32[]{:S(2)}, u32[]{:S(2)}) collective-permute-start(bf16[192,1152]{1,0:T(8,128)(2,1)S(1)} %collective-permute-done.2.between_ref), channel_id=1, source_target_pairs={{8,0},{12,4},{16,24},{20,28},{9,1},{13,5},{17,25},{21,29},{10,2},{... | collective-permute-start | bytes 1327112 | tf_op jit(solution)/shard_map/end_mid/ppermute | solution.py:403
  17.6 0.7 collective-permute-start.6
  18.3 0.0 copy-start
  18.3 1.7 %copy-done = bf16[1,768,1536]{2,1,0:T(8,128)(2,1)S(1)} copy-done((bf16[1,768,1536]{2,1,0:T(8,128)(2,1)S(1)}, bf16[1,768,1536]{2,1,0:T(8,128)(2,1)}, u32[]{:S(2)}) %copy-start) | copy-done | bytes 2359320
  19.9 0.1 take_tail.1
  20.1 0.0 copy-start.1
  20.1 6.6 %collective-permute-done.3.refs_3_ = bf16[192,1152]{1,0:T(8,128)(2,1)S(1)} collective-permute-done((bf16[192,1152]{1,0:T(8,128)(2,1)S(1)}, bf16[192,1152]{1,0:T(8,128)(2,1)S(1)}, u32[]{:S(2)}, u32[]{:S(2)}) %collective-permute-start.3) | collective-permute-done | bytes 442400 | tf_op jit(solution)/shard_map/near_across/ppermute | solution.py:409
  26.6 4.3 %collective-permute-done.4.end_ref = bf16[192,1152]{1,0:T(8,128)(2,1)S(1)} collective-permute-done((bf16[192,1152]{1,0:T(8,128)(2,1)S(1)}, bf16[192,1152]{1,0:T(8,128)(2,1)S(1)}, u32[]{:S(2)}, u32[]{:S(2)}) %collective-permute-start.4) | collective-permute-done | bytes 442400 | tf_op jit(solution)/shard_map/end_mid/ppermute | solution.py:403
  31.0 0.0 collective-permute-done.6.between_ref
  31.0 0.8 collective-permute-start.10
  31.7 0.3 choose.2.refs_4_
  32.0 1.3 %collective-permute-start.7 = (bf16[192,1152]{1,0:T(8,128)(2,1)S(1)}, bf16[192,1152]{1,0:T(8,128)(2,1)S(1)}, u32[]{:S(2)}, u32[]{:S(2)}) collective-permute-start(bf16[192,1152]{1,0:T(8,128)(2,1)S(1)} %collective-permute-done.6.between_ref), channel_id=1, source_target_pairs={{8,0},{12,4},{16,24},{20,28},{9,1},{13,5},{17,25},{21,29},{10,2},{... | collective-permute-start | bytes 1327112 | tf_op jit(solution)/shard_map/end_far/ppermute | solution.py:403
  33.3 1.6 %collective-permute-start.5 = (bf16[192,1152]{1,0:T(8,128)(2,1)S(1)}, bf16[192,1152]{1,0:T(8,128)(2,1)S(1)}, u32[]{:S(2)}, u32[]{:S(2)}) collective-permute-start(bf16[192,1152]{1,0:T(8,128)(2,1)S(1)} %choose.2.refs_4_), channel_id=1, source_target_pairs={{0,4},{4,0},{8,12},{12,8},{16,20},{20,16},{24,28},{28,24},{1,5},{5... | collective-permute-start | bytes 1327112 | tf_op jit(solution)/shard_map/second_across/ppermute | solution.py:409
  34.9 12.3 %collective-permute-done.7.end_ref = bf16[192,1152]{1,0:T(8,128)(2,1)S(1)} collective-permute-done((bf16[192,1152]{1,0:T(8,128)(2,1)S(1)}, bf16[192,1152]{1,0:T(8,128)(2,1)S(1)}, u32[]{:S(2)}, u32[]{:S(2)}) %collective-permute-start.7) | collective-permute-done | bytes 442400 | tf_op jit(solution)/shard_map/end_far/ppermute | solution.py:403
  47.2 0.3 choose.3.refs_6_
  47.5 0.0 copy-start.3
  47.5 0.0 copy-start.4
  47.5 0.0 copy-start.5
  47.5 0.0 collective-permute-done.5.refs_5_
  47.5 1.6 %collective-permute-start.8 = (bf16[192,1152]{1,0:T(8,128)(2,1)S(1)}, bf16[192,1152]{1,0:T(8,128)(2,1)S(1)}, u32[]{:S(2)}, u32[]{:S(2)}) collective-permute-start(bf16[192,1152]{1,0:T(8,128)(2,1)S(1)} %choose.3.refs_6_), channel_id=1, source_target_pairs={{0,4},{4,0},{8,12},{12,8},{16,20},{20,16},{24,28},{28,24},{1,5},{5... | collective-permute-start | bytes 1327112 | tf_op jit(solution)/shard_map/third_across/ppermute | solution.py:409
  49.1 0.0 collective-permute-done.9.refs_7_.refs_9_
  49.1 0.0 copy-done.1
  49.1 7.8 %project_early.1 = (f32[768,1152]{1,0:T(8,128)S(1)}, f32[768,1152]{1,0:T(8,128)S(1)}) custom-call(bf16[192,1152]{1,0:T(8,128)(2,1)S(1)} %take_half.1.refs_0_, bf16[192,1152]{1,0:T(8,128)(2,1)S(1)} %collective-permute-done.refs_1_, bf16[192,1152]{1,0:T(8,128)(2,1)S(1)} %collective-permute-done.1.refs_2_, ...), custom_call_target="tpu_custom_call" | custom-call | tf_op jit(solution)/shard_map/project_early/pallas_call | solution.py:299
  57.0 2.1 %collective-permute-done.8.refs_7_ = bf16[192,1152]{1,0:T(8,128)(2,1)S(1)} collective-permute-done((bf16[192,1152]{1,0:T(8,128)(2,1)S(1)}, bf16[192,1152]{1,0:T(8,128)(2,1)S(1)}, u32[]{:S(2)}, u32[]{:S(2)}) %collective-permute-start.8) | collective-permute-done | bytes 442400 | tf_op jit(solution)/shard_map/third_across/ppermute | solution.py:409
  59.0 0.0 collective-permute-done.10.refs_10_
  59.0 1.3 %collective-permute-start.11 = (bf16[512,1536]{1,0:T(8,128)(2,1)S(1)}, bf16[512,1536]{1,0:T(8,128)(2,1)S(1)}, u32[]{:S(2)}, u32[]{:S(2)}) collective-permute-start(bf16[512,1536]{1,0:T(8,128)(2,1)S(1)} %collective-permute-done.10.refs_10_), channel_id=1, source_target_pairs={{1,0},{3,2},{5,4},{7,6},{9,8},{11,10},{13,12},{15,14},{17,16},{19,... | collective-permute-start | bytes 4718600 | tf_op jit(solution)/shard_map/halo_first/ppermute | solution.py:479
  60.3 0.0 copy-done.3
  60.3 0.0 copy-done.4
  60.3 0.0 copy-done.5
  60.3 8.0 %project_late_attend.1 = (bf16[1024,384]{1,0:T(8,128)(2,1)S(1)}, bf16[1536,384]{1,0:T(8,128)(2,1)S(1)}, bf16[2048,384]{1,0:T(8,128)(2,1)S(1)}, bf16[2048,384]{1,0:T(8,128)(2,1)S(1)}, bf16[1536,768]{1,0:T(8,128)(2,1)S(1)}) custom-call(s32[1,3]{1,0:T(1,128)S(1)} %copy-done.3, s32[1,12]{1,0:T(1,128)S(1)} %copy-done.4, s32[1,12]{1,0:T(1,128)S(1)} %copy-done.5, ...), custom_call_target="tpu_custom_call" | custom-call | tf_op jit(solution)/shard_map/project_late_attend/pallas_call | solution.py:340
  68.3 1.9 %collective-permute-start.12 = (bf16[1024,384]{1,0:T(8,128)(2,1)S(1)}, bf16[1024,384]{1,0:T(8,128)(2,1)S(1)}, u32[]{:S(2)}, u32[]{:S(2)}) collective-permute-start(bf16[1024,384]{1,0:T(8,128)(2,1)S(1)} %get-tuple-element.32.done_ref), channel_id=1, source_target_pairs={{0,1},{1,0},{2,3},{3,2},{4,5},{5,4},{6,7},{7,6},{8,9},{9,8},{10,11... | collective-permute-start | bytes 2359304 | tf_op jit(solution)/shard_map/swap/ppermute | solution.py:486
  70.2 0.0 collective-permute-done.11.halo_ref
  70.2 4.4 %attend_own.1.own_ref = bf16[768,384]{1,0:T(8,128)(2,1)S(1)} custom-call(s32[1,3]{1,0:T(1,128)S(1)} %copy-done.3, s32[1,12]{1,0:T(1,128)S(1)} %copy-done.4, s32[1,12]{1,0:T(1,128)S(1)} %copy-done.5, bf16[1536,384]{1,0:T(8,128)(2,1)S(1)} %get-tuple-element.27.q_ref, bf16[2048,384]{1,0:T(8,128)(2,1)S(1)} %get-tuple-element.28.k_ref, ...), custom_call_target="tpu_custom_call" | custom-call | tf_op jit(solution)/shard_map/attend_own/pallas_call | solution.py:365
  74.6 0.0 collective-permute-done.12.other_ref
  74.7 1.0 %join.1 = bf16[768,768]{1,0:T(8,128)(2,1)} custom-call(bf16[768,384]{1,0:T(8,128)(2,1)S(1)} %attend_own.1.own_ref, bf16[1024,384]{1,0:T(8,128)(2,1)S(1)} %collective-permute-done.12.other_ref), custom_call_target="tpu_custom_call" | custom-call | tf_op jit(solution)/shard_map/join/pallas_call | solution.py:283
Async XLA Ops:
  0.0 1.2 %copy-start.2 = (bf16[192,2304]{1,0:T(8,128)(2,1)S(1)}, bf16[192,2304]{1,0:T(8,128)(2,1)}, u32[]{:S(2)}) copy-start(bf16[192,2304]{1,0:T(8,128)(2,1)} %w_ref.1) | copy-start | bytes 2654212
  1.3 13.2 %collective-permute-start = (bf16[192,1152]{1,0:T(8,128)(2,1)S(1)}, bf16[192,1152]{1,0:T(8,128)(2,1)S(1)}, u32[]{:S(2)}, u32[]{:S(2)}) collective-permute-start(bf16[192,1152]{1,0:T(8,128)(2,1)S(1)} %take_half.1.refs_0_), channel_id=1, source_target_pairs={{0,4},{4,0},{8,12},{12,8},{16,20},{20,16},{24,28},{28,24},{1,5},{5... | collective-permute-start | bytes 1327112 | tf_op jit(solution)/shard_map/half_across/ppermute | solution.py:409
  4.3 11.6 %collective-permute-start.1 = (bf16[192,1152]{1,0:T(8,128)(2,1)S(1)}, bf16[192,1152]{1,0:T(8,128)(2,1)S(1)}, u32[]{:S(2)}, u32[]{:S(2)}) collective-permute-start(bf16[192,1152]{1,0:T(8,128)(2,1)S(1)} %take_half.1.refs_0_), channel_id=1, source_target_pairs={{8,0},{12,4},{16,24},{20,28},{0,8},{4,12},{24,16},{28,20},{9,1},{1... | collective-permute-start | bytes 1327112 | tf_op jit(solution)/shard_map/near/ppermute | solution.py:403
  5.9 10.1 %collective-permute-start.2 = (bf16[192,1152]{1,0:T(8,128)(2,1)S(1)}, bf16[192,1152]{1,0:T(8,128)(2,1)S(1)}, u32[]{:S(2)}, u32[]{:S(2)}) collective-permute-start(bf16[192,1152]{1,0:T(8,128)(2,1)S(1)} %take_half.1.refs_0_), channel_id=1, source_target_pairs={{8,16},{12,20},{16,8},{20,12},{9,17},{13,21},{17,9},{21,13},{10,18... | collective-permute-start | bytes 1327112 | tf_op jit(solution)/shard_map/mid/ppermute | solution.py:403
  6.5 42.6 %collective-permute-start.9 = (bf16[768,1536]{1,0:T(8,128)(2,1)}, bf16[768,1536]{1,0:T(8,128)(2,1)S(1)}, u32[]{:S(2)}, u32[]{:S(2)}) collective-permute-start(bf16[768,1536]{1,0:T(8,128)(2,1)} %bitcast.2), channel_id=1, source_target_pairs={{0,1},{1,0},{2,3},{3,2},{4,5},{5,4},{6,7},{7,6},{8,9},{9,8},{10,11... | collective-permute-start | bytes 7077896 | tf_op jit(solution)/shard_map/partner/ppermute | solution.py:461
  15.9 10.7 %collective-permute-start.3 = (bf16[192,1152]{1,0:T(8,128)(2,1)S(1)}, bf16[192,1152]{1,0:T(8,128)(2,1)S(1)}, u32[]{:S(2)}, u32[]{:S(2)}) collective-permute-start(bf16[192,1152]{1,0:T(8,128)(2,1)S(1)} %collective-permute-done.1.refs_2_), channel_id=1, source_target_pairs={{0,4},{4,0},{8,12},{12,8},{16,20},{20,16},{24,28},{28,24},{1,5},{5... | collective-permute-start | bytes 1327112 | tf_op jit(solution)/shard_map/near_across/ppermute | solution.py:409
  16.3 14.7 %collective-permute-start.4 = (bf16[192,1152]{1,0:T(8,128)(2,1)S(1)}, bf16[192,1152]{1,0:T(8,128)(2,1)S(1)}, u32[]{:S(2)}, u32[]{:S(2)}) collective-permute-start(bf16[192,1152]{1,0:T(8,128)(2,1)S(1)} %collective-permute-done.2.between_ref), channel_id=1, source_target_pairs={{8,0},{12,4},{16,24},{20,28},{9,1},{13,5},{17,25},{21,29},{10,2},{... | collective-permute-start | bytes 1327112 | tf_op jit(solution)/shard_map/end_mid/ppermute | solution.py:403
  17.6 13.4 %collective-permute-start.6 = (bf16[192,1152]{1,0:T(8,128)(2,1)S(1)}, bf16[192,1152]{1,0:T(8,128)(2,1)S(1)}, u32[]{:S(2)}, u32[]{:S(2)}) collective-permute-start(bf16[192,1152]{1,0:T(8,128)(2,1)S(1)} %collective-permute-done.1.refs_2_), channel_id=1, source_target_pairs={{8,16},{12,20},{16,8},{20,12},{9,17},{13,21},{17,9},{21,13},{10,18... | collective-permute-start | bytes 1327112 | tf_op jit(solution)/shard_map/mid_far/ppermute | solution.py:403
  18.3 1.7 %copy-start = (bf16[1,768,1536]{2,1,0:T(8,128)(2,1)S(1)}, bf16[1,768,1536]{2,1,0:T(8,128)(2,1)}, u32[]{:S(2)}) copy-start(bf16[1,768,1536]{2,1,0:T(8,128)(2,1)} %param.5) | copy-start | bytes 7077892
  20.1 29.1 %copy-start.1 = (bf16[1,768,1536]{2,1,0:T(8,128)(2,1)S(1)}, bf16[1,768,1536]{2,1,0:T(8,128)(2,1)}, u32[]{:S(2)}) copy-start(bf16[1,768,1536]{2,1,0:T(8,128)(2,1)} %param.5) | copy-start | bytes 7077892
  31.0 28.0 %collective-permute-start.10 = (bf16[512,1536]{1,0:T(8,128)(2,1)S(1)}, bf16[512,1536]{1,0:T(8,128)(2,1)S(1)}, u32[]{:S(2)}, u32[]{:S(2)}) collective-permute-start(bf16[512,1536]{1,0:T(8,128)(2,1)S(1)} %take_tail.1), channel_id=1, source_target_pairs={{1,3},{5,7},{9,11},{13,15},{17,19},{21,23},{25,27},{29,31}} | collective-permute-start | bytes 4718600 | tf_op jit(solution)/shard_map/halo/ppermute | solution.py:472
  32.0 15.2 %collective-permute-start.7 = (bf16[192,1152]{1,0:T(8,128)(2,1)S(1)}, bf16[192,1152]{1,0:T(8,128)(2,1)S(1)}, u32[]{:S(2)}, u32[]{:S(2)}) collective-permute-start(bf16[192,1152]{1,0:T(8,128)(2,1)S(1)} %collective-permute-done.6.between_ref), channel_id=1, source_target_pairs={{8,0},{12,4},{16,24},{20,28},{9,1},{13,5},{17,25},{21,29},{10,2},{... | collective-permute-start | bytes 1327112 | tf_op jit(solution)/shard_map/end_far/ppermute | solution.py:403
  33.3 14.2 %collective-permute-start.5 = (bf16[192,1152]{1,0:T(8,128)(2,1)S(1)}, bf16[192,1152]{1,0:T(8,128)(2,1)S(1)}, u32[]{:S(2)}, u32[]{:S(2)}) collective-permute-start(bf16[192,1152]{1,0:T(8,128)(2,1)S(1)} %choose.2.refs_4_), channel_id=1, source_target_pairs={{0,4},{4,0},{8,12},{12,8},{16,20},{20,16},{24,28},{28,24},{1,5},{5... | collective-permute-start | bytes 1327112 | tf_op jit(solution)/shard_map/second_across/ppermute | solution.py:409
  47.5 12.8 %copy-start.3 = (s32[1,3]{1,0:T(1,128)S(1)}, s32[1,3]{1,0:T(1,128)}, u32[]{:S(2)}) copy-start(s32[1,3]{1,0:T(1,128)} %start_ref.3) | copy-start | bytes 40
  47.5 12.8 %copy-start.4 = (s32[1,12]{1,0:T(1,128)S(1)}, s32[1,12]{1,0:T(1,128)}, u32[]{:S(2)}) copy-start(s32[1,12]{1,0:T(1,128)} %owner_ref.3) | copy-start | bytes 148
  47.5 12.8 %copy-start.5 = (s32[1,12]{1,0:T(1,128)S(1)}, s32[1,12]{1,0:T(1,128)}, u32[]{:S(2)}) copy-start(s32[1,12]{1,0:T(1,128)} %left_ref.3) | copy-start | bytes 148
  47.5 11.5 %collective-permute-start.8 = (bf16[192,1152]{1,0:T(8,128)(2,1)S(1)}, bf16[192,1152]{1,0:T(8,128)(2,1)S(1)}, u32[]{:S(2)}, u32[]{:S(2)}) collective-permute-start(bf16[192,1152]{1,0:T(8,128)(2,1)S(1)} %choose.3.refs_6_), channel_id=1, source_target_pairs={{0,4},{4,0},{8,12},{12,8},{16,20},{20,16},{24,28},{28,24},{1,5},{5... | collective-permute-start | bytes 1327112 | tf_op jit(solution)/shard_map/third_across/ppermute | solution.py:409
  59.0 11.2 %collective-permute-start.11 = (bf16[512,1536]{1,0:T(8,128)(2,1)S(1)}, bf16[512,1536]{1,0:T(8,128)(2,1)S(1)}, u32[]{:S(2)}, u32[]{:S(2)}) collective-permute-start(bf16[512,1536]{1,0:T(8,128)(2,1)S(1)} %collective-permute-done.10.refs_10_), channel_id=1, source_target_pairs={{1,0},{3,2},{5,4},{7,6},{9,8},{11,10},{13,12},{15,14},{17,16},{19,... | collective-permute-start | bytes 4718600 | tf_op jit(solution)/shard_map/halo_first/ppermute | solution.py:479
  68.3 6.3 %collective-permute-start.12 = (bf16[1024,384]{1,0:T(8,128)(2,1)S(1)}, bf16[1024,384]{1,0:T(8,128)(2,1)S(1)}, u32[]{:S(2)}, u32[]{:S(2)}) collective-permute-start(bf16[1024,384]{1,0:T(8,128)(2,1)S(1)} %get-tuple-element.32.done_ref), channel_id=1, source_target_pairs={{0,1},{1,0},{2,3},{3,2},{4,5},{5,4},{6,7},{7,6},{8,9},{9,8},{10,11... | collective-permute-start | bytes 2359304 | tf_op jit(solution)/shard_map/swap/ppermute | solution.py:486
